TPU v7x, 512 devices: a whole 4x4x16 slice. The times are simulated.
512 devices in a mesh: layer: 8 (over y, core), tile: 64 (over z, x).
Axes of the slice: x: 4, y: 4, z: 16, core: 2. Of those that a mesh axis runs over, the one named last changes fastest.
Arguments:
- cond_x: float32 [8, 256, 2048], P(None, 'tile', 'layer'), may hold values from 0.3 to 3
- cond_y: float32 [8, 256, 2048], P(None, 'tile', 'layer'), may hold values from 0.3 to 3
- via_cond: float32 [8, 256, 2048], P(None, 'tile', 'layer'), may hold values from 0.5 to 4
- capacity: float32 [8, 256, 2048], P(None, 'tile', 'layer'), may hold values from 0.002 to 0.02
- class_map: int32 [256, 2048], P('tile', 'layer'), may hold values from 0 to 7
- via_mask: int32 [8, 8], replicated, may hold values 0 or 1
- bank_map: int32 [8, 64, 128], P(None, 'tile', 'layer'), may hold values from 0 to 255
- source_late: float32 [8, 256, 2048], P(None, 'tile', 'layer'), may hold values from -6 to 6
- source_early: float32 [8, 256, 2048], P(None, 'tile', 'layer'), may hold values from -6 to 6
- rate_late: float32 [8, 256, 2048], P(None, 'tile', 'layer'), may hold values from -6 to 6
- rate_early: float32 [8, 256, 2048], P(None, 'tile', 'layer'), may hold values from -6 to 6
Outputs:
- adjoint_late: float32 [8, 256, 2048], P(None, 'tile', 'layer')
- adjoint_early: float32 [8, 256, 2048], P(None, 'tile', 'layer')
- bank_grad: float32 [256], replicated
All inputs are finite; a program needn't handle non-finite values.
Results may differ from a plain program's by a relative error of at most 0.0003.
Values sent between devices are 32-bit elements; how exact they have to be, the bound alone decides.
A program may use at most 64 MiB of HBM per device.

v0:
```python
from functools import partial

import jax
import jax.numpy as jnp
from jax import lax
from jax.sharding import PartitionSpec as P

ITERS = 3
CHEB = 4
NCLASS = 8
DROWS = 4
DCOLS = 16
BANKS = 256


lower_edge = 0.05
upper_edge = 2.0
centre_value = (lower_edge + upper_edge) / 2.0
half_width = (upper_edge - lower_edge) / 2.0
sigma_value = centre_value / half_width


def shifted(value, axis, by):
    peers = lax.axis_size(axis)
    pairs = [(i, i + by) for i in range(peers) if 0 <= i + by < peers]
    return lax.ppermute(value, axis, pairs)


def padded_2(cells, sides, width):
    for axis, dim in sides:
        count = lax.axis_size(axis)
        ends = count - 1
        head = lax.slice_in_dim(cells, 0, width, axis=dim)
        tail = lax.slice_in_dim(cells, cells.shape[dim] - width, cells.shape[dim], axis=dim)
        cells = jnp.concatenate(
            [
                lax.ppermute(tail, axis, [(i, (i + 1) % count) for i in range(ends)]),
                cells,
                lax.ppermute(head, axis, [((i + 1) % count, i) for i in range(ends)]),
            ],
            axis=dim,
        )
    return cells


def couplings(cond_x, cond_y, via_cond, capacity, class_map, via_mask):
    last_band = lax.axis_index("layer") == lax.axis_size("layer") - 1
    last_strip = lax.axis_index("tile") == lax.axis_size("tile") - 1
    east = jnp.where(last_band, cond_x.at[:, :, -1].set(0.0), cond_x)
    came_left = shifted(east[:, :, -1:], "layer", 1)
    west = jnp.concatenate([came_left, east[:, :, :-1]], axis=2)
    south = jnp.where(last_strip, cond_y.at[:, -1, :].set(0.0), cond_y)
    came_above = shifted(south[:, -1:, :], "tile", 1)
    north = jnp.concatenate([came_above, south[:, :-1, :]], axis=1)
    classes = jnp.arange(NCLASS, dtype=jnp.int32)
    onehot = (class_map[None] == classes[:, None, None]).astype(jnp.float32)
    opened = jnp.tensordot(
        via_mask.astype(jnp.float32), onehot, axes=((1,), (0,)), precision=lax.Precision.HIGHEST
    )
    upward = (via_cond * opened).at[-1].set(0.0)
    downward = jnp.pad(upward[:-1], ((1, 0), (0, 0), (0, 0)))
    diagonal = capacity + east + west + south + north + upward + downward
    return (east, west, south, north, upward, downward, diagonal)


def apply_stencil(field, padded, coefs):
    east, west, south, north, upward, downward, diagonal = coefs
    result = diagonal * field - east * padded[1:-1, 1:-1, 2:] - west * padded[1:-1, 1:-1, :-2]
    result = result - south * padded[1:-1, 2:, 1:-1] - north * padded[1:-1, :-2, 1:-1]
    return result - upward * padded[2:, 1:-1, 1:-1] - downward * padded[:-2, 1:-1, 1:-1]


def operate(field, coefs):
    framed = padded_2(field, (("layer", 2), ("tile", 1)), 1)
    padded = jnp.pad(framed, ((1, 1), (0, 0), (0, 0)))
    return apply_stencil(field, padded, coefs)


def chebyshev(residual, diagonal, coefs, stencil):
    smooth = residual / (centre_value * diagonal)
    step_dir = smooth
    rho_prev = 1.0 / sigma_value
    for sweep in range(CHEB - 1):
        rho_next = 1.0 / (2.0 * sigma_value - rho_prev)
        step_dir = (
            rho_next * rho_prev * step_dir
            + 2.0 * rho_next / half_width * (residual - stencil(smooth, coefs)) / diagonal
        )
        smooth = smooth + step_dir
        rho_prev = rho_next
    return smooth


def precondition(residual, coefs):
    return chebyshev(residual, coefs[6], coefs, operate)


def single_product(first, second):
    return lax.psum(jnp.sum(first * second), ("layer", "tile"))


def solve(rhs, coefs, apply_m):
    solution = jnp.zeros_like(rhs)
    residual = rhs
    precond = apply_m(residual)
    search = precond
    gamma = single_product(residual, precond)
    for step in range(ITERS):
        image = operate(search, coefs)
        alpha = gamma / single_product(search, image)
        solution = solution + alpha * search
        residual = residual - alpha * image
        if step + 1 < ITERS:
            precond = apply_m(residual)
            gamma_next = single_product(residual, precond)
            search = precond + gamma_next / gamma * search
            gamma = gamma_next
    return solution


def on_device(
    cond_x,
    cond_y,
    via_cond,
    capacity,
    class_map,
    via_mask,
    bank_map,
    source_late,
    source_early,
    rate_late,
    rate_early,
):
    coefs = couplings(cond_x, cond_y, via_cond, capacity, class_map, via_mask)
    apply_m = partial(precondition, coefs=coefs)
    adjoint_late = solve(source_late, coefs, apply_m)
    adjoint_early = solve(source_early + capacity * adjoint_late, coefs, apply_m)
    product = adjoint_late * rate_late + adjoint_early * rate_early
    layer_count, row_count, col_count = product.shape
    tiles = (
        product.reshape(layer_count, row_count // DROWS, DROWS, col_count // DCOLS, DCOLS)
        .sum(axis=(2, 4))
        .reshape(-1)
    )
    banks = jnp.arange(BANKS, dtype=jnp.int32)
    onehot = (bank_map.reshape(-1)[:, None] == banks[None, :]).astype(jnp.float32)
    partial_sums = jnp.dot(tiles, onehot, precision=lax.Precision.HIGHEST)
    bank_grad = lax.psum(partial_sums, ("layer", "tile"))
    return (adjoint_late, adjoint_early, bank_grad)


def solution(mesh):
    in_specs = (
        P(None, "tile", "layer"),
        P(None, "tile", "layer"),
        P(None, "tile", "layer"),
        P(None, "tile", "layer"),
        P("tile", "layer"),
        P(),
        P(None, "tile", "layer"),
        P(None, "tile", "layer"),
        P(None, "tile", "layer"),
        P(None, "tile", "layer"),
        P(None, "tile", "layer"),
    )
    out_specs = (P(None, "tile", "layer"), P(None, "tile", "layer"), P())
    return jax.shard_map(
        on_device, mesh=mesh, in_specs=in_specs, out_specs=out_specs, check_vma=False
    )
```

profile of v0, /device:TPU:1, one launch (start us, length us, event | category | flops | bytes accessed | tf_op | source)
XLA Modules:
  0.0 1590.9 jit_solution(2470584285932996485)
XLA Ops:
  26.8 5.2 collective-permute-start.7
  34.3 4.5 collective-permute-start.9
  41.9 5.1 collective-permute-start.11
  49.1 4.5 collective-permute-start.13
  56.7 5.1 collective-permute-start.15
  64.0 4.5 collective-permute-start.17
  70.2 124.3 %all-reduce.26 = (f32[]{:T(128)}, f32[]{:T(128)}) all-reduce(f32[]{:T(128)} %get-tuple-element.48, f32[]{:T(128)} %get-tuple-element.47), channel_id=1, replica_groups=mesh['layer'=8,'tile'=64] {'layer','tile'}, use_global_device_ids=true, to_apply=%region_1.2 | all-reduce | flops 2 | bytes 16 | tf_op jit(solution)/shard_map/psum | solution.py:99
  211.5 4.6 collective-permute-start.23
  218.4 4.5 collective-permute-start.25
  226.0 5.1 collective-permute-start.27
  233.3 4.5 collective-permute-start.29
  239.5 112.5 %psum.93 = f32[]{:T(128)} all-reduce(f32[]{:T(128)} %get-tuple-element.91), channel_id=1, replica_groups=mesh['layer'=8,'tile'=64] {'layer','tile'}, use_global_device_ids=true, to_apply=%region_5.6 | all-reduce | flops 1 | bytes 8 | tf_op jit(solution)/shard_map/psum | solution.py:99
  366.8 106.7 %psum.94 = f32[]{:T(128)} all-reduce(f32[]{:T(128)} %get-tuple-element.89), channel_id=1, replica_groups=mesh['layer'=8,'tile'=64] {'layer','tile'}, use_global_device_ids=true, to_apply=%region_7.8 | all-reduce | flops 1 | bytes 8 | tf_op jit(solution)/shard_map/psum | solution.py:99
  497.3 4.5 collective-permute-start.41
  504.9 5.1 collective-permute-start.43
  512.2 4.5 collective-permute-start.45
  518.4 112.7 %psum.95 = f32[]{:T(128)} all-reduce(f32[]{:T(128)} %get-tuple-element.81), channel_id=1, replica_groups=mesh['layer'=8,'tile'=64] {'layer','tile'}, use_global_device_ids=true, to_apply=%region_9.10 | all-reduce | flops 1 | bytes 8 | tf_op jit(solution)/shard_map/psum | solution.py:99
  646.0 106.7 %psum.96 = f32[]{:T(128)} all-reduce(f32[]{:T(128)} %fusion.167), channel_id=1, replica_groups=mesh['layer'=8,'tile'=64] {'layer','tile'}, use_global_device_ids=true, to_apply=%region_11.12 | all-reduce | flops 1 | bytes 8 | tf_op jit(solution)/shard_map/psum | solution.py:99
  769.7 4.6 collective-permute-start.55
  784.1 5.1 collective-permute-start.59
  799.0 5.1 collective-permute-start.63
  806.3 4.7 collective-permute-start.65
  812.6 116.0 %all-reduce.25 = (f32[]{:T(128)}, f32[]{:T(128)}) all-reduce(f32[]{:T(128)} %get-tuple-element.46, f32[]{:T(128)} %get-tuple-element.45), channel_id=1, replica_groups=mesh['layer'=8,'tile'=64] {'layer','tile'}, use_global_device_ids=true, to_apply=%region_13.14 | all-reduce | flops 2 | bytes 16 | tf_op jit(solution)/shard_map/psum | solution.py:99
  945.5 4.8 collective-permute-start.71
  960.1 5.1 collective-permute-start.75
  973.6 113.1 %psum.99 = f32[]{:T(128)} all-reduce(f32[]{:T(128)} %get-tuple-element.65), channel_id=1, replica_groups=mesh['layer'=8,'tile'=64] {'layer','tile'}, use_global_device_ids=true, to_apply=%region_17.18 | all-reduce | flops 1 | bytes 8 | tf_op jit(solution)/shard_map/psum | solution.py:99
  1101.6 106.1 %psum.100 = f32[]{:T(128)} all-reduce(f32[]{:T(128)} %get-tuple-element.63), channel_id=1, replica_groups=mesh['layer'=8,'tile'=64] {'layer','tile'}, use_global_device_ids=true, to_apply=%region_19.20 | all-reduce | flops 1 | bytes 8 | tf_op jit(solution)/shard_map/psum | solution.py:99
  1224.4 4.8 collective-permute-start.87
  1239.0 5.1 collective-permute-start.91
  1252.5 113.2 %psum.101 = f32[]{:T(128)} all-reduce(f32[]{:T(128)} %get-tuple-element.55), channel_id=1, replica_groups=mesh['layer'=8,'tile'=64] {'layer','tile'}, use_global_device_ids=true, to_apply=%region_21.22 | all-reduce | flops 1 | bytes 8 | tf_op jit(solution)/shard_map/psum | solution.py:99
  1381.9 106.1 %psum.102 = f32[]{:T(128)} all-reduce(f32[]{:T(128)} %fusion.6), channel_id=1, replica_groups=mesh['layer'=8,'tile'=64] {'layer','tile'}, use_global_device_ids=true, to_apply=%region_23.24 | all-reduce | flops 1 | bytes 8 | tf_op jit(solution)/shard_map/psum | solution.py:99
  1489.8 100.5 %psum.103 = f32[256]{0:T(256)} all-reduce(f32[256]{0:T(256)S(1)} %bitcast.37), channel_id=1, replica_groups=mesh['layer'=8,'tile'=64] {'layer','tile'}, use_global_device_ids=true, to_apply=%region_26.27 | all-reduce | flops 256 | bytes 2048 | tf_op jit(solution)/shard_map/psum | solution.py:148
  (320 shorter events, 256.3 us)
Async XLA Ops:
  1.4 10.3 collective-permute-start.1
  5.5 6.2 collective-permute-start
  24.8 7.3 collective-permute-start.6
  26.8 6.0 collective-permute-start.7
  33.0 5.8 collective-permute-start.8
  39.9 7.0 collective-permute-start.10
  41.9 5.9 collective-permute-start.11
  47.9 5.8 collective-permute-start.12
  54.8 7.0 collective-permute-start.14
  56.7 5.9 collective-permute-start.15
  62.7 5.8 collective-permute-start.16
  208.9 7.3 collective-permute-start.22
  217.1 5.8 collective-permute-start.24
  224.1 7.0 collective-permute-start.26
  226.0 5.9 collective-permute-start.27
  487.8 7.3 collective-permute-start.38
  496.0 5.8 collective-permute-start.40
  503.0 7.0 collective-permute-start.42
  504.9 5.9 collective-permute-start.43
  767.0 7.3 collective-permute-start.54
  782.2 7.0 collective-permute-start.58
  784.1 5.9 collective-permute-start.59
  797.1 7.0 collective-permute-start.62
  799.0 5.9 collective-permute-start.63
  805.0 6.0 collective-permute-start.64
  943.0 7.3 collective-permute-start.70
  958.2 7.0 collective-permute-start.74
  960.1 5.9 collective-permute-start.75
  1222.0 7.3 collective-permute-start.86
  1237.1 7.0 collective-permute-start.90
  1239.0 5.9 collective-permute-start.91
  1373.7 6.7 collective-permute-start.96
  (76 other events, 690.7 us)
where the time goes:
time: 1600 us; the launch traced here: 1590 us
  blocking collectives  1220 us (76%)
  starting transfers between devices  297 us (19%)
  waiting for transfers between devices  40.2 us (3%)
    psum x10, blocking collectives, single_product(): return lax.psum(jnp.sum(first * second), ('layer', 'tile'))  1120 us
    ppermute x48, starting transfers between devices, padded_2(): lax.ppermute(tail, axis, [(i, (i + 1) % count) for i in range(ends)])  201 us
    psum x1, blocking collectives, on_device(): bank_grad = lax.psum(partial_sums, ('layer', 'tile'))  100 us
    ppermute x48, starting transfers between devices, padded_2(): lax.ppermute(head, axis, [((i + 1) % count, i) for i in range(ends)])  88 us
    ppermute x48, waiting for transfers between devices, padded_2(): lax.ppermute(tail, axis, [(i, (i + 1) % count) for i in range(ends)])  38.6 us
  transfers between devices with their start and end apart: 98, of which 48 were waited for; matrix products, arithmetic and copies ran while one was open for 0% of the time, Pallas kernels for 0%

commit v1 on v0

v1 whole, which is shorter than its diff:
```python
import functools

import jax
import jax.numpy as jnp
from jax import lax
from jax.experimental import pallas as pl
from jax.experimental.pallas import tpu as pltpu
from jax.sharding import PartitionSpec as P

MESH = pl.DeviceIdType.MESH
NCLASS = 8
DCOLS = 16
BANKS = 256
LAYERS = 8
ROWS = 4
COLS = 256
HALO = 4
SPAN = ROWS + 2 * HALO
WIDE = COLS + 128
FIELDS = 6
EAST, SOUTH, UP, CAP, LATE, EARLY = range(FIELDS)

lower_edge = 0.05
upper_edge = 2.0
centre = (lower_edge + upper_edge) / 2.0
half = (upper_edge - lower_edge) / 2.0
sigma = centre / half


def sweep_constants():
    out = []
    rho = 1.0 / sigma
    for _ in range(3):
        nxt = 1.0 / (2.0 * sigma - rho)
        out.append((nxt * rho, 2.0 * nxt / half))
        rho = nxt
    return out


def next_col(v):
    return pltpu.roll(v, WIDE - 1, 1)


def prev_col(v):
    return pltpu.roll(v, 1, 1)


def next_layer(v):
    return pltpu.roll(v, LAYERS - 1, 0)


def prev_layer(v):
    return pltpu.roll(v, 1, 0)


def neighbours(z, coef, r):
    v = z[r]
    acc = coef[0, r] * next_col(v) + coef[1, r] * prev_col(v)
    acc = acc + (coef[2, r] * z[r + 1] + coef[3, r] * z[r - 1])
    return acc + (coef[4, r] * next_layer(v) + coef[5, r] * prev_layer(v))


def krylov_coefficients(mu):
    zero = jnp.zeros_like(mu[0])
    one = zero + 1.0

    def form(c, base):
        total = None
        for s in range(2 * len(c) - 1):
            w = None
            for i in range(len(c)):
                j = s - i
                if 0 <= j < len(c):
                    w = c[i] * c[j] if w is None else w + c[i] * c[j]
            total = w * mu[base + s] if total is None else total + w * mu[base + s]
        return total

    res = [one]
    sea = [one]
    sol = [zero, zero, zero]
    gamma = mu[0]
    for step in range(3):
        alpha = gamma / form(sea, 1)
        sol = [s + alpha * sea[i] if i < len(sea) else s for i, s in enumerate(sol)]
        if step < 2:
            res = [
                (res[i] if i < len(res) else zero) - (alpha * sea[i - 1] if i > 0 else zero)
                for i in range(step + 2)
            ]
            new = form(res, 0)
            beta = new / gamma
            sea = [res[i] + (beta * sea[i] if i < len(sea) else zero) for i in range(step + 2)]
            gamma = new
    return sol


def kernel(
    cond_x, cond_y, via, cap, cls, mask, bank, late, early, rate_late, rate_early,
    out_late, out_early, out_bank,
    ext, col_r, col_l, sx, sx_r, sx_l, coef, diag, g, u, uh, z1, z2,
    a0, a1, a2, b0, b1, b2,
    halo_send, halo_recv, mid_send, mid_recv, ush_send, ush_recv, sum_send, sum_recv,
):
    lay = lax.axis_index("layer")
    til = lax.axis_index("tile")
    lays = lax.axis_size("layer")
    tils = lax.axis_size("tile")
    y, core = lay // 2, lay % 2
    z, x = til // 4, til % 4

    def at(dl, dt):
        return ((lay + dl + lays) % lays, (til + dt + tils) % tils)

    core_peer = [(lay + 1 - 2 * core, til)]
    plane_peers = [
        (((y + i // 4) % 4) * 2 + core, z * 4 + (x + i) % 4) for i in range(1, 16)
    ]
    z_peers = [(lay, ((z + i) % 16) * 4 + x) for i in range(1, 16)]

    barrier = pltpu.get_barrier_semaphore()
    greet = [at(dl, dt) for dt in (-2, -1, 0, 1, 2) for dl in (-1, 0, 1) if (dl, dt) != (0, 0)]
    greet += plane_peers + z_peers
    for d in greet:
        pl.semaphore_signal(barrier, inc=1, device_id=d, device_id_type=MESH)

    lane = lax.broadcasted_iota(jnp.int32, (LAYERS, COLS), 1)
    layer = lax.broadcasted_iota(jnp.int32, (LAYERS, COLS), 0)
    last_col = jnp.logical_and(lane == COLS - 1, lay == lays - 1)
    top = layer == LAYERS - 1
    masks = mask[...].astype(jnp.float32)
    for r in range(ROWS):
        e = HALO + r
        ext[EAST, e, :, :COLS] = jnp.where(last_col, 0.0, cond_x[:, r, :])
        south = cond_y[:, r, :]
        if r == ROWS - 1:
            south = jnp.where(til == tils - 1, 0.0, south)
        ext[SOUTH, e, :, :COLS] = south
        kind = jnp.broadcast_to(cls[r : r + 1, :], (LAYERS, COLS))
        opened = jnp.zeros((LAYERS, COLS), jnp.float32)
        for k in range(NCLASS):
            opened = jnp.where(kind == k, masks[:, k : k + 1], opened)
        ext[UP, e, :, :COLS] = jnp.where(top, 0.0, via[:, r, :] * opened)
        ext[CAP, e, :, :COLS] = cap[:, r, :]
        ext[LATE, e, :, :COLS] = late[:, r, :]
        ext[EARLY, e, :, :COLS] = early[:, r, :]

    pl.semaphore_wait(barrier, len(greet))

    own = pl.ds(HALO, ROWS)
    halo = []

    def send(src, dst, peer):
        n = len(halo)
        halo.append(
            pltpu.make_async_remote_copy(
                src_ref=src, dst_ref=dst, send_sem=halo_send.at[n], recv_sem=halo_recv.at[n],
                device_id=peer, device_id_type=MESH,
            )
        )
        halo[-1].start()

    for dt, row in ((1, 0), (-1, HALO + ROWS)):
        send(ext.at[:, own, :, pl.ds(0, COLS)], ext.at[:, pl.ds(row, HALO), :, pl.ds(0, COLS)], at(0, dt))
    for dt, row in ((1, 0), (-1, HALO + ROWS), (0, HALO)):
        send(ext.at[:, own, :, pl.ds(0, 128)], col_r.at[:, pl.ds(row, HALO)], at(-1, dt))
        send(ext.at[:, own, :, pl.ds(COLS - 128, 128)], col_l.at[:, pl.ds(row, HALO)], at(1, dt))
    far = ext.at[SOUTH, HALO + ROWS - 1]
    send(far.at[:, pl.ds(0, COLS)], sx.at[:, pl.ds(0, COLS)], at(0, 2))
    send(far.at[:, pl.ds(0, 128)], sx_r, at(-1, 2))
    send(far.at[:, pl.ds(COLS - 128, 128)], sx_l, at(1, 2))
    for c in halo:
        c.wait_recv()

    right = lax.broadcasted_iota(jnp.int32, (LAYERS, 128), 1) < 64
    for f in range(FIELDS):
        for r in range(SPAN):
            ext[f, r, :, COLS:] = jnp.where(right, col_r[f, r], col_l[f, r])
    north = jnp.concatenate([sx[...], jnp.where(right, sx_r[...], sx_l[...])], axis=1)
    for r in range(SPAN):
        east = ext[EAST, r]
        west = prev_col(east)
        south = ext[SOUTH, r]
        upward = ext[UP, r]
        downward = prev_layer(upward)
        d = ext[CAP, r] + east + west + south + north + upward + downward
        inv = 1.0 / d
        diag[0, r] = d
        diag[1, r] = inv
        g[0, r] = ext[LATE, r] * inv
        for i, c in enumerate((east, west, south, north, upward, downward)):
            coef[i, r] = c * inv
        north = south

    (q1, p1), (q2, p2), (q3, p3) = sweep_constants()

    def smooth(gi, ui):
        for r in range(1, SPAN - 1):
            z1[r] = ((1.0 + q1 - p1) / centre + p1) * gi[r] + (p1 / centre) * neighbours(gi, coef, r)
        for r in range(2, SPAN - 2):
            z2[r] = (1.0 + q2 - p2) * z1[r] + (p2 - q2 / centre) * gi[r] + p2 * neighbours(z1, coef, r)
        for r in range(3, SPAN - 3):
            ui[r] = (
                (1.0 + q3 - p3) * z2[r] - q3 * z1[r] + p3 * gi[r] + p3 * neighbours(z2, coef, r)
            )

    def rows_both_ways(ref, above, below, ssem, rsem):
        copies = []
        for n, (dt, dst) in enumerate(((1, above), (-1, below))):
            c = pltpu.make_async_remote_copy(
                src_ref=ref.at[own], dst_ref=dst,
                send_sem=ssem.at[n], recv_sem=rsem.at[n], device_id=at(0, dt), device_id_type=MESH,
            )
            c.start()
            copies.append(c)
        return copies

    pending = []

    def chain(base):
        parts = [None] * 6
        for i in range(3):
            gi, ui = g.at[base + i], u.at[base + i]
            smooth(gi, ui)
            gn = g.at[base + i + 1] if i < 2 else z1
            for r in range(HALO, HALO + ROWS):
                gn[r] = ui[r] - neighbours(ui, coef, r)
            if i < 2:
                k = base // 3 * 2 + i
                copies = rows_both_ways(
                    gn, gn.at[pl.ds(0, HALO)], gn.at[pl.ds(HALO + ROWS, HALO)],
                    mid_send.at[k], mid_recv.at[k],
                )
                pending.extend(copies)
            for r in range(HALO, HALO + ROWS):
                du = (diag[0, r] * ui[r])[:, :COLS]
                for k, ref in ((2 * i, gi), (2 * i + 1, gn)):
                    term = du * ref[r][:, :COLS]
                    parts[k] = term if parts[k] is None else parts[k] + term
            if i < 2:
                for c in copies:
                    c.wait_recv()
        lanes = lax.broadcasted_iota(jnp.int32, (1, 128), 1)
        row = jnp.zeros((1, 128), jnp.float32)
        for k, p in enumerate(parts):
            row = jnp.where(lanes == k, jnp.sum(p, axis=(0, 1), keepdims=True), row)
        return row

    def group_sum(buf, me, peers, n, ssem, rsem):
        for d in peers:
            pltpu.make_async_remote_copy(
                src_ref=buf.at[me], dst_ref=buf.at[me], send_sem=ssem, recv_sem=rsem,
                device_id=d, device_id_type=MESH,
            ).start()
        most = buf.at[pl.ds(0, n - 1)]
        whole = pltpu.make_async_remote_copy(
            src_ref=most, dst_ref=most, send_sem=ssem, recv_sem=rsem,
            device_id=peers[0], device_id_type=MESH,
        )
        whole.wait_recv()
        pending.append(whole)
        total = buf[0]
        for i in range(1, n):
            total = total + buf[i]
        return total

    def all_sum(bufs, base):
        c, p, w = bufs
        p[y * 4 + x] = group_sum(c, core, core_peer, 2, sum_send.at[base], sum_recv.at[base])
        w[z] = group_sum(p, y * 4 + x, plane_peers, 16, sum_send.at[base + 1], sum_recv.at[base + 1])
        return group_sum(w, z, z_peers, 16, sum_send.at[base + 2], sum_recv.at[base + 2])

    def coefficients(row):
        lanes = lax.broadcasted_iota(jnp.int32, (1, 128), 1)
        mu = [
            jnp.sum(jnp.where(lanes == k, row, 0.0), axis=(0, 1), keepdims=True) for k in range(6)
        ]
        return krylov_coefficients(mu)

    a0[core] = chain(0).reshape(1, 1, 128)
    for i in range(3):
        copies = rows_both_ways(
            u.at[i], uh.at[i, pl.ds(0, HALO)], uh.at[i, pl.ds(HALO, HALO)],
            ush_send.at[i], ush_recv.at[i],
        )
        pending.extend(copies)
    shadow = pending[-6:]
    c1 = coefficients(all_sum((a0, a1, a2), 0).reshape(1, 128))
    for c in shadow:
        c.wait_recv()
    held = jnp.zeros((LAYERS, COLS), jnp.float32)
    for r in range(SPAN):
        inside = HALO <= r < HALO + ROWS
        src, s = (u, r) if inside else (uh, r if r < HALO else r - ROWS)
        v = c1[0] * src[0, s] + c1[1] * src[1, s] + c1[2] * src[2, s]
        g[3, r] = (ext[EARLY, r] + ext[CAP, r] * v) * diag[1, r]
        if inside:
            out_late[:, r - HALO, :] = v[:, :COLS]
            held = held + v[:, :COLS] * rate_late[:, r - HALO, :]

    moments = chain(3)
    terms = [held]
    for i in range(3):
        t = None
        for r in range(ROWS):
            w = u[3 + i, HALO + r][:, :COLS] * rate_early[:, r, :]
            t = w if t is None else t + w
        terms.append(t)

    hi = lax.Precision.HIGHEST
    f32 = jnp.float32

    def iota(shape, dim):
        return lax.broadcasted_iota(jnp.int32, shape, dim)

    spread = (iota((16, 128), 0) == iota((16, 128), 1) % 16).astype(f32)
    bank_of = jnp.dot(bank[...].astype(f32), spread, precision=hi, preferred_element_type=f32)
    mine = iota((LAYERS, 128), 0) == iota((LAYERS, 128), 1) // 16
    bank_row = jnp.sum(jnp.where(mine, bank_of, 0.0), axis=0, keepdims=True)
    chosen = (iota((BANKS, 128), 0) == (bank_row + 0.5).astype(jnp.int32)).astype(f32)
    tile_of = (iota((COLS, 128), 0) // DCOLS == iota((COLS, 128), 1) % 16).astype(f32)
    tiles = jnp.dot(jnp.concatenate(terms, axis=0), tile_of, precision=hi, preferred_element_type=f32)
    tiles = jnp.where(iota((4 * LAYERS, 128), 0) % LAYERS == iota((4 * LAYERS, 128), 1) // 16, tiles, 0.0)
    sums = lax.dot_general(
        tiles, chosen, (((1,), (1,)), ((), ())), precision=hi, preferred_element_type=f32
    )
    for i in range(4):
        s = jnp.sum(sums[i * LAYERS : (i + 1) * LAYERS], axis=0, keepdims=True)
        b0[core, 2 * i] = s[:, :128]
        b0[core, 2 * i + 1] = s[:, 128:]
    b0[core, 8] = moments

    total = all_sum((b0, b1, b2), 3)
    c2 = coefficients(total[8])
    for h in range(2):
        out_bank[:, h * 128 : (h + 1) * 128] = (
            total[h] + c2[0] * total[2 + h] + c2[1] * total[4 + h] + c2[2] * total[6 + h]
        )
    for r in range(ROWS):
        e = HALO + r
        v = c2[0] * u[3, e] + c2[1] * u[4, e] + c2[2] * u[5, e]
        out_early[:, r, :] = v[:, :COLS]
    for c in halo:
        c.wait_send()
    for c in pending:
        c.wait_send()


def on_device(
    cond_x, cond_y, via_cond, capacity, class_map, via_mask, bank_map,
    source_late, source_early, rate_late, rate_early,
):
    f32 = jnp.float32
    vm = pl.BlockSpec(memory_space=pltpu.VMEM)
    dma = pltpu.SemaphoreType.DMA
    block = jax.ShapeDtypeStruct((LAYERS, ROWS, COLS), f32)
    wide = (SPAN, LAYERS, WIDE)
    late, early, bank = pl.pallas_call(
        kernel,
        out_shape=(block, block, jax.ShapeDtypeStruct((1, BANKS), f32)),
        in_specs=[vm] * 11,
        out_specs=(vm, vm, vm),
        scratch_shapes=[
            pltpu.VMEM((FIELDS,) + wide, f32),
            pltpu.VMEM((FIELDS, SPAN, LAYERS, 128), f32),
            pltpu.VMEM((FIELDS, SPAN, LAYERS, 128), f32),
            pltpu.VMEM((LAYERS, COLS), f32),
            pltpu.VMEM((LAYERS, 128), f32),
            pltpu.VMEM((LAYERS, 128), f32),
            pltpu.VMEM((6,) + wide, f32),
            pltpu.VMEM((2,) + wide, f32),
            pltpu.VMEM((6,) + wide, f32),
            pltpu.VMEM((6,) + wide, f32),
            pltpu.VMEM((3, 2 * HALO, LAYERS, WIDE), f32),
            pltpu.VMEM(wide, f32),
            pltpu.VMEM(wide, f32),
            pltpu.VMEM((2, 1, 1, 128), f32),
            pltpu.VMEM((16, 1, 1, 128), f32),
            pltpu.VMEM((16, 1, 1, 128), f32),
            pltpu.VMEM((2, 9, 1, 128), f32),
            pltpu.VMEM((16, 9, 1, 128), f32),
            pltpu.VMEM((16, 9, 1, 128), f32),
            dma((11,)),
            dma((11,)),
            dma((4, 2)),
            dma((4, 2)),
            dma((3, 2)),
            dma((3, 2)),
            dma((6,)),
            dma((6,)),
        ],
        compiler_params=pltpu.CompilerParams(
            collective_id=0, has_side_effects=True, vmem_limit_bytes=40 << 20
        ),
        name="adjoint_steps",
    )(
        cond_x, cond_y, via_cond, capacity, class_map, via_mask, bank_map.reshape(LAYERS, 16),
        source_late, source_early, rate_late, rate_early,
    )
    return late, early, bank.reshape(BANKS)


def solution(mesh):
    block = P(None, "tile", "layer")
    in_specs = (block,) * 4 + (P("tile", "layer"), P()) + (block,) * 5
    return jax.shard_map(
        on_device, mesh=mesh, in_specs=in_specs, out_specs=(block, block, P()), check_vma=False
    )
```

time: 1600 us -> 86.7 us (0.05)
  blocking collectives: 1220 us -> 0 us
  starting transfers between devices: 297 us -> 0 us
  Pallas kernels: 0 us -> 75.1 us
  waiting for transfers between devices: 40.2 us -> 0 us
    psum x11 -> x0, blocking collectives: 1220 us -> none  [the longest x10 1120 us: single_product(): return lax.psum(jnp.sum(first * second), ('layer', 'tile'))]
    ppermute x98 -> x0, starting transfers between devices: 297 us -> none  [the longest x48 201 us: padded_2(): lax.ppermute(tail, axis, [(i, (i + 1) % count) for i in range(ends)])]
    pallas_call x0 -> x1, Pallas kernels: none -> 75.1 us  [on_device(): pl.pallas_call(kernel, out_shape=(block, block, jax.ShapeDtypeStruct((1,...]
    ppermute x98 -> x0, waiting for transfers between devices: 40.2 us -> none  [the longest x48 38.6 us: padded_2(): lax.ppermute(tail, axis, [(i, (i + 1) % count) for i in range(ends)])]
  transfers between devices with their start and end apart: 98 -> 0, of which waited for: 48 -> 0; matrix products, arithmetic and copies ran while one was open for 0% -> 0% of each run, Pallas kernels for 0% -> 0%
where the time goes in v1:
time: 86.7 us; the launch traced here: 85.7 us
  Pallas kernels  75.1 us (87%)
  local copies, waits for them, and re-layouts  9.91 us (11%)
    pallas_call x1, Pallas kernels, on_device(): pl.pallas_call(kernel, out_shape=(block, block, jax.ShapeDtypeStruct((1,...  75.1 us
    unnamed x25, local copies, waits for them, and re-layouts  9.91 us

profile of v1, /device:TPU:1, one launch (start us, length us, event | category | flops | bytes accessed | tf_op | source)
XLA Modules:
  0.0 85.7 jit_solution(592809720669880522)
XLA Ops:
  0.6 0.0 copy-start
  0.6 0.7 copy-done
  1.4 0.0 copy-start.1
  1.4 0.8 copy-done.1
  2.2 0.0 copy-start.2
  2.2 0.8 copy-done.2
  2.9 0.0 copy-start.3
  2.9 0.8 copy-done.3
  3.7 0.0 copy-start.4
  3.7 0.8 copy-done.4
  4.4 0.0 copy-start.5
  4.4 0.8 copy-done.5
  5.2 0.0 copy-start.6
  5.2 0.8 copy-done.6
  5.9 0.0 copy-start.7
  5.9 0.8 copy-done.7
  6.7 0.0 copy-start.8
  6.7 0.7 copy-done.8
  7.4 0.0 copy-start.9
  7.4 0.7 copy-done.9
  8.1 0.0 copy-start.10
  8.1 0.7 copy-done.10
  8.8 75.1 %adjoint_steps.1 = (f32[8,4,256]{2,1,0:T(4,128)S(1)}, f32[8,4,256]{2,1,0:T(4,128)S(1)}, f32[1,256]{1,0:T(1,128)S(1)}) custom-call(f32[8,4,256]{2,1,0:T(4,128)S(1)} %copy-done, f32[8,4,256]{2,1,0:T(4,128)S(1)} %copy-done.1, f32[8,4,256]{2,1,0:T(4,128)S(1)} %copy-done.2, f32[8,4,256]{2,1,0:T(4,128)S(1)} %copy-done.3, s32[4,256]{1,0:T(4,128)S(1)} %copy-done.8, ...), custom_call_target="tpu_custom_call" | custom-call | tf_op jit(solution)/shard_map/adjoint_steps/pallas_call | solution.py:357
  83.9 0.6 copy.17
  84.5 0.6 copy.18
  85.1 0.6 copy.19
Async XLA Ops:
  0.6 0.8 copy-start
  1.4 0.8 copy-start.1
  2.2 0.8 copy-start.2
  2.9 0.8 copy-start.3
  3.7 0.8 copy-start.4
  4.4 0.8 copy-start.5
  5.2 0.8 copy-start.6
  5.9 0.8 copy-start.7
  6.7 0.7 copy-start.8
  7.4 0.7 copy-start.9
  8.1 0.7 copy-start.10

commit v2 on v1

--- a/solution.py
+++ b/solution.py
@@ -63,8 +63,9 @@
 def krylov_coefficients(mu):
     zero = jnp.zeros_like(mu[0])
     one = zero + 1.0
-
-    def form(c, base):
+    nu = [mu[s] - mu[s + 1] for s in range(5)]
+
+    def form(c, moments):
         total = None
         for s in range(2 * len(c) - 1):
             w = None
@@ -72,35 +73,46 @@
                 j = s - i
                 if 0 <= j < len(c):
                     w = c[i] * c[j] if w is None else w + c[i] * c[j]
-            total = w * mu[base + s] if total is None else total + w * mu[base + s]
+            total = w * moments[s] if total is None else total + w * moments[s]
         return total
 
-    res = [one]
-    sea = [one]
-    sol = [zero, zero, zero]
+    def plus(a, b, scale):
+        n = max(len(a), len(b))
+        a, b = a + [zero] * (n - len(a)), b + [zero] * (n - len(b))
+        return [p + scale * q for p, q in zip(a, b)]
+
+    res, sea, sol = [one], [one], []
     gamma = mu[0]
     for step in range(3):
-        alpha = gamma / form(sea, 1)
-        sol = [s + alpha * sea[i] if i < len(sea) else s for i, s in enumerate(sol)]
+        alpha = gamma / form(sea, nu)
+        sol = plus(sol, sea, alpha)
         if step < 2:
-            res = [
-                (res[i] if i < len(res) else zero) - (alpha * sea[i - 1] if i > 0 else zero)
-                for i in range(step + 2)
-            ]
-            new = form(res, 0)
-            beta = new / gamma
-            sea = [res[i] + (beta * sea[i] if i < len(sea) else zero) for i in range(step + 2)]
+            res = plus(plus(res, sea, -alpha), [zero] + sea, alpha)
+            new = form(res, mu)
+            sea = plus(res, sea, new / gamma)
             gamma = new
     return sol
 
 
 def kernel(
-    cond_x, cond_y, via, cap, cls, mask, bank, late, early, rate_late, rate_early,
-    out_late, out_early, out_bank,
+    cond_x_in, cond_y_in, via_in, cap_in, cls_in, mask_in, bank_in, late_in, early_in, rate_late_in, rate_early_in,
+    late_out, early_out, bank_out,
+    out_late, out_early, out_bank, cond_x, cond_y, via, cap, cls, mask, bank, late, early, rate_late, rate_early,
     ext, col_r, col_l, sx, sx_r, sx_l, coef, diag, g, u, uh, z1, z2,
     a0, a1, a2, b0, b1, b2,
-    halo_send, halo_recv, mid_send, mid_recv, ush_send, ush_recv, sum_send, sum_recv,
+    load_sem, store_sem, halo_send, halo_recv, mid_send, mid_recv, ush_send, ush_recv, sum_send, sum_recv, reach,
 ):
+    loads = [
+        pltpu.make_async_copy(src, dst, load_sem.at[n])
+        for n, (src, dst) in enumerate((
+            (cond_x_in, cond_x), (cond_y_in, cond_y), (via_in, via), (cap_in, cap), (cls_in, cls),
+            (mask_in, mask), (late_in, late), (early_in, early), (bank_in, bank),
+            (rate_late_in, rate_late), (rate_early_in, rate_early),
+        ))
+    ]
+    for c in loads:
+        c.start()
+
     lay = lax.axis_index("layer")
     til = lax.axis_index("tile")
     lays = lax.axis_size("layer")
@@ -119,7 +131,7 @@
 
     barrier = pltpu.get_barrier_semaphore()
     greet = [at(dl, dt) for dt in (-2, -1, 0, 1, 2) for dl in (-1, 0, 1) if (dl, dt) != (0, 0)]
-    greet += plane_peers + z_peers
+    greet += plane_peers + [at(0, 4 * dz) for dz in (-2, -1, 1, 2)]
     for d in greet:
         pl.semaphore_signal(barrier, inc=1, device_id=d, device_id_type=MESH)
 
@@ -127,6 +139,8 @@
     layer = lax.broadcasted_iota(jnp.int32, (LAYERS, COLS), 0)
     last_col = jnp.logical_and(lane == COLS - 1, lay == lays - 1)
     top = layer == LAYERS - 1
+    for c in loads[:8]:
+        c.wait()
     masks = mask[...].astype(jnp.float32)
     for r in range(ROWS):
         e = HALO + r
@@ -145,6 +159,8 @@
         ext[EARLY, e, :, :COLS] = early[:, r, :]
 
     pl.semaphore_wait(barrier, len(greet))
+    for dz in (-2, 2):
+        pl.semaphore_signal(reach.at[0], inc=1, device_id=at(0, 4 * dz), device_id_type=MESH)
 
     own = pl.ds(HALO, ROWS)
     halo = []
@@ -159,22 +175,42 @@
         )
         halo[-1].start()
 
-    for dt, row in ((1, 0), (-1, HALO + ROWS)):
-        send(ext.at[:, own, :, pl.ds(0, COLS)], ext.at[:, pl.ds(row, HALO), :, pl.ds(0, COLS)], at(0, dt))
-    for dt, row in ((1, 0), (-1, HALO + ROWS), (0, HALO)):
-        send(ext.at[:, own, :, pl.ds(0, 128)], col_r.at[:, pl.ds(row, HALO)], at(-1, dt))
-        send(ext.at[:, own, :, pl.ds(COLS - 128, 128)], col_l.at[:, pl.ds(row, HALO)], at(1, dt))
+    def send_fields(first, count):
+        fields = pl.ds(first, count)
+        for dt, row in ((1, 0), (-1, HALO + ROWS)):
+            send(
+                ext.at[fields, own, :, pl.ds(0, COLS)],
+                ext.at[fields, pl.ds(row, HALO), :, pl.ds(0, COLS)],
+                at(0, dt),
+            )
+        for dt, row in ((1, 0), (-1, HALO + ROWS), (0, HALO)):
+            send(ext.at[fields, own, :, pl.ds(0, 128)], col_r.at[fields, pl.ds(row, HALO)], at(-1, dt))
+            send(
+                ext.at[fields, own, :, pl.ds(COLS - 128, 128)],
+                col_l.at[fields, pl.ds(row, HALO)],
+                at(1, dt),
+            )
+
+    send_fields(0, EARLY)
     far = ext.at[SOUTH, HALO + ROWS - 1]
     send(far.at[:, pl.ds(0, COLS)], sx.at[:, pl.ds(0, COLS)], at(0, 2))
     send(far.at[:, pl.ds(0, 128)], sx_r, at(-1, 2))
     send(far.at[:, pl.ds(COLS - 128, 128)], sx_l, at(1, 2))
-    for c in halo:
+    first = len(halo)
+    send_fields(EARLY, 1)
+    for c in halo[:first]:
         c.wait_recv()
+    pl.semaphore_wait(reach.at[0], 2)
+    for dz in (-4, 4):
+        pl.semaphore_signal(reach.at[1], inc=1, device_id=at(0, 4 * dz), device_id_type=MESH)
 
     right = lax.broadcasted_iota(jnp.int32, (LAYERS, 128), 1) < 64
-    for f in range(FIELDS):
+    def merge_columns(f):
         for r in range(SPAN):
             ext[f, r, :, COLS:] = jnp.where(right, col_r[f, r], col_l[f, r])
+
+    for f in range(EARLY):
+        merge_columns(f)
     north = jnp.concatenate([sx[...], jnp.where(right, sx_r[...], sx_l[...])], axis=1)
     for r in range(SPAN):
         east = ext[EAST, r]
@@ -223,7 +259,7 @@
             smooth(gi, ui)
             gn = g.at[base + i + 1] if i < 2 else z1
             for r in range(HALO, HALO + ROWS):
-                gn[r] = ui[r] - neighbours(ui, coef, r)
+                gn[r] = gi[r] - ui[r] + neighbours(ui, coef, r)
             if i < 2:
                 k = base // 3 * 2 + i
                 copies = rows_both_ways(
@@ -284,6 +320,12 @@
         )
         pending.extend(copies)
     shadow = pending[-6:]
+    for c in halo[first:]:
+        c.wait_recv()
+    merge_columns(EARLY)
+    pl.semaphore_wait(reach.at[1], 2)
+    for c in loads[8:10]:
+        c.wait()
     c1 = coefficients(all_sum((a0, a1, a2), 0).reshape(1, 128))
     for c in shadow:
         c.wait_recv()
@@ -297,6 +339,16 @@
             out_late[:, r - HALO, :] = v[:, :COLS]
             held = held + v[:, :COLS] * rate_late[:, r - HALO, :]
 
+    stores = [
+        pltpu.make_async_copy(src, dst, store_sem.at[n])
+        for n, (src, dst) in enumerate(
+            ((out_late, late_out), (out_early, early_out), (out_bank, bank_out))
+        )
+    ]
+    stores[0].start()
+
+    for c in loads[10:]:
+        c.wait()
     moments = chain(3)
     terms = [held]
     for i in range(3):
@@ -339,27 +391,50 @@
         e = HALO + r
         v = c2[0] * u[3, e] + c2[1] * u[4, e] + c2[2] * u[5, e]
         out_early[:, r, :] = v[:, :COLS]
+    stores[1].start()
+    stores[2].start()
     for c in halo:
         c.wait_send()
     for c in pending:
         c.wait_send()
+    for c in stores:
+        c.wait()
+
+
+def finish(late, early, bank, out_late, out_early, out_bank, sem):
+    copies = [
+        pltpu.make_async_copy(src, dst, sem.at[n])
+        for n, (src, dst) in enumerate(((late, out_late), (early, out_early), (bank, out_bank)))
+    ]
+    for c in copies:
+        c.start()
+    for c in copies:
+        c.wait()
 
 
 def on_device(
     cond_x, cond_y, via_cond, capacity, class_map, via_mask, bank_map,
     source_late, source_early, rate_late, rate_early,
 ):
-    f32 = jnp.float32
-    vm = pl.BlockSpec(memory_space=pltpu.VMEM)
+    f32, i32 = jnp.float32, jnp.int32
+    hbm = pl.BlockSpec(memory_space=pltpu.HBM)
     dma = pltpu.SemaphoreType.DMA
     block = jax.ShapeDtypeStruct((LAYERS, ROWS, COLS), f32)
+    shapes = (block, block, jax.ShapeDtypeStruct((1, BANKS), f32))
     wide = (SPAN, LAYERS, WIDE)
-    late, early, bank = pl.pallas_call(
+    field = pltpu.VMEM((LAYERS, ROWS, COLS), f32)
+    results = pl.pallas_call(
         kernel,
-        out_shape=(block, block, jax.ShapeDtypeStruct((1, BANKS), f32)),
-        in_specs=[vm] * 11,
-        out_specs=(vm, vm, vm),
+        out_shape=shapes,
+        in_specs=[hbm] * 11,
+        out_specs=(hbm,) * 3,
         scratch_shapes=[
+            field, field, pltpu.VMEM((1, BANKS), f32),
+            field, field, field, field,
+            pltpu.VMEM((ROWS, COLS), i32),
+            pltpu.VMEM((LAYERS, NCLASS), i32),
+            pltpu.VMEM((LAYERS, 16), i32),
+            field, field, field, field,
             pltpu.VMEM((FIELDS,) + wide, f32),
             pltpu.VMEM((FIELDS, SPAN, LAYERS, 128), f32),
             pltpu.VMEM((FIELDS, SPAN, LAYERS, 128), f32),
@@ -380,22 +455,34 @@
             pltpu.VMEM((16, 9, 1, 128), f32),
             pltpu.VMEM((16, 9, 1, 128), f32),
             dma((11,)),
-            dma((11,)),
+            dma((3,)),
+            dma((19,)),
+            dma((19,)),
             dma((4, 2)),
             dma((4, 2)),
             dma((3, 2)),
             dma((3, 2)),
             dma((6,)),
             dma((6,)),
+            pltpu.SemaphoreType.REGULAR((2,)),
         ],
         compiler_params=pltpu.CompilerParams(
-            collective_id=0, has_side_effects=True, vmem_limit_bytes=40 << 20
+            collective_id=0, has_side_effects=True, vmem_limit_bytes=60 << 20
         ),
         name="adjoint_steps",
     )(
         cond_x, cond_y, via_cond, capacity, class_map, via_mask, bank_map.reshape(LAYERS, 16),
         source_late, source_early, rate_late, rate_early,
     )
+    late, early, bank = pl.pallas_call(
+        finish,
+        out_shape=shapes,
+        in_specs=[hbm] * 3,
+        out_specs=(hbm,) * 3,
+        scratch_shapes=[dma((3,))],
+        compiler_params=pltpu.CompilerParams(vmem_limit_bytes=60 << 20),
+        name="write_results",
+    )(*results)
     return late, early, bank.reshape(BANKS)
 
 

time: 86.7 us -> 76.5 us (0.88)
  local copies, waits for them, and re-layouts: 9.91 us -> 0 us
    unnamed x25 -> x0, local copies, waits for them, and re-layouts: 9.91 us -> none
    pallas_call x1 -> x2, Pallas kernels: 75.1 us -> 75.6 us  [the longest x1 72.5 us: on_device(): pl.pallas_call(kernel, out_shape=shapes, in_specs=[hbm] * 11, out_specs=(...]
where the time goes in v2:
time: 76.5 us; the launch traced here: 76.3 us
  Pallas kernels  75.6 us (99%)
    pallas_call x1, Pallas kernels, on_device(): pl.pallas_call(kernel, out_shape=shapes, in_specs=[hbm] * 11, out_specs=(...  72.5 us
    pallas_call x1, Pallas kernels, on_device(): pl.pallas_call(finish, out_shape=shapes, in_specs=[hbm] * 3, out_specs=(h...  3.15 us

profile of v2, /device:TPU:1, one launch (start us, length us, event | category | flops | bytes accessed | tf_op | source)
XLA Modules:
  0.0 76.3 jit_solution(7429135966308976484)
XLA Ops:
  0.6 72.5 %adjoint_steps.1 = (f32[8,4,256]{2,1,0:T(4,128)}, f32[8,4,256]{2,1,0:T(4,128)}, f32[1,256]{1,0:T(1,128)}) custom-call(f32[8,4,256]{2,1,0:T(4,128)} %cond_x_in.1, f32[8,4,256]{2,1,0:T(4,128)} %cond_y_in.1, f32[8,4,256]{2,1,0:T(4,128)} %via_in.1, f32[8,4,256]{2,1,0:T(4,128)} %cap_in.1, s32[4,256]{1,0:T(4,128)} %cls_in.1, s32[8,8]{1,0:T(8,128)} %mask_in.1, ...), custom_call_target="tpu_custom_call" | custom-call | tf_op jit(solution)/shard_map/adjoint_steps/pallas_call | solution.py:426
  73.1 3.1 %write_results.1 = (f32[8,4,256]{2,1,0:T(4,128)}, f32[8,4,256]{2,1,0:T(4,128)}, f32[1,256]{1,0:T(1,128)}) custom-call(f32[8,4,256]{2,1,0:T(4,128)} %get-tuple-element.9.late, f32[8,4,256]{2,1,0:T(4,128)} %get-tuple-element.10.early, f32[1,256]{1,0:T(1,128)} %get-tuple-element.11.bank), custom_call_target="tpu_custom_call" | custom-call | tf_op jit(solution)/shard_map/write_results/pallas_call | solution.py:477

commit v3 on v2

--- a/solution.py
+++ b/solution.py
@@ -14,9 +14,11 @@
 LAYERS = 8
 ROWS = 4
 COLS = 256
-HALO = 4
+HALO = 8
+NEAR = 4
 SPAN = ROWS + 2 * HALO
 WIDE = COLS + 128
+EDGE = 24
 FIELDS = 6
 EAST, SOUTH, UP, CAP, LATE, EARLY = range(FIELDS)
 
@@ -98,7 +100,7 @@
     cond_x_in, cond_y_in, via_in, cap_in, cls_in, mask_in, bank_in, late_in, early_in, rate_late_in, rate_early_in,
     late_out, early_out, bank_out,
     out_late, out_early, out_bank, cond_x, cond_y, via, cap, cls, mask, bank, late, early, rate_late, rate_early,
-    ext, col_r, col_l, sx, sx_r, sx_l, coef, diag, g, u, uh, z1, z2,
+    ext, pack_r, pack_l, col_r, col_l, early_r, early_l, sx, sx_r, sx_l, coef, diag, g, u, uh, z1, z2,
     a0, a1, a2, b0, b1, b2,
     load_sem, store_sem, halo_send, halo_recv, mid_send, mid_recv, ush_send, ush_recv, sum_send, sum_recv, reach,
 ):
@@ -125,13 +127,16 @@
 
     core_peer = [(lay + 1 - 2 * core, til)]
     plane_peers = [
-        (((y + i // 4) % 4) * 2 + core, z * 4 + (x + i) % 4) for i in range(1, 16)
+        (((y + dy) % 4) * 2 + core, z * 4 + (x + dx) % 4)
+        for dy in (2, 1, 3, 0) for dx in (2, 1, 3, 0) if (dy, dx) != (0, 0)
     ]
-    z_peers = [(lay, ((z + i) % 16) * 4 + x) for i in range(1, 16)]
+    z_peers = [
+        (lay, ((z + i) % 16) * 4 + x) for i in sorted(range(1, 16), key=lambda i: -min(i, 16 - i))
+    ]
 
     barrier = pltpu.get_barrier_semaphore()
     greet = [at(dl, dt) for dt in (-2, -1, 0, 1, 2) for dl in (-1, 0, 1) if (dl, dt) != (0, 0)]
-    greet += plane_peers + [at(0, 4 * dz) for dz in (-2, -1, 1, 2)]
+    greet += plane_peers + [at(0, 4 * dz) for dz in (-2, 2, -1, 1)]
     for d in greet:
         pl.semaphore_signal(barrier, inc=1, device_id=d, device_id_type=MESH)
 
@@ -157,6 +162,17 @@
         ext[CAP, e, :, :COLS] = cap[:, r, :]
         ext[LATE, e, :, :COLS] = late[:, r, :]
         ext[EARLY, e, :, :COLS] = early[:, r, :]
+        lane128 = lax.broadcasted_iota(jnp.int32, (LAYERS, 128), 1)
+        right = jnp.zeros((LAYERS, 128), jnp.float32)
+        left = right
+        for f in range(EARLY):
+            here = jnp.logical_and(lane128 >= EDGE * f, lane128 < EDGE * (f + 1))
+            v = ext[f, e, :, :128]
+            right = jnp.where(here, pltpu.roll(v, EDGE * f, 1) if f else v, right)
+            v = ext[f, e, :, COLS - 128 : COLS]
+            left = jnp.where(here, pltpu.roll(v, (EDGE * (f + 1)) % 128, 1), left)
+        pack_r[r] = right
+        pack_l[r] = left
 
     pl.semaphore_wait(barrier, len(greet))
     for dz in (-2, 2):
@@ -175,104 +191,144 @@
         )
         halo[-1].start()
 
-    def send_fields(first, count):
+    def send_rows(first, count, dt, row):
         fields = pl.ds(first, count)
-        for dt, row in ((1, 0), (-1, HALO + ROWS)):
-            send(
-                ext.at[fields, own, :, pl.ds(0, COLS)],
-                ext.at[fields, pl.ds(row, HALO), :, pl.ds(0, COLS)],
-                at(0, dt),
-            )
-        for dt, row in ((1, 0), (-1, HALO + ROWS), (0, HALO)):
-            send(ext.at[fields, own, :, pl.ds(0, 128)], col_r.at[fields, pl.ds(row, HALO)], at(-1, dt))
-            send(
-                ext.at[fields, own, :, pl.ds(COLS - 128, 128)],
-                col_l.at[fields, pl.ds(row, HALO)],
-                at(1, dt),
-            )
-
-    send_fields(0, EARLY)
-    far = ext.at[SOUTH, HALO + ROWS - 1]
-    send(far.at[:, pl.ds(0, COLS)], sx.at[:, pl.ds(0, COLS)], at(0, 2))
-    send(far.at[:, pl.ds(0, 128)], sx_r, at(-1, 2))
-    send(far.at[:, pl.ds(COLS - 128, 128)], sx_l, at(1, 2))
+        send(
+            ext.at[fields, own, :, pl.ds(0, COLS)],
+            ext.at[fields, pl.ds(row, ROWS), :, pl.ds(0, COLS)],
+            at(0, dt),
+        )
+
+    def send_columns(dt, row):
+        send(pack_r, col_r.at[pl.ds(row, ROWS)], at(-1, dt))
+        send(pack_l, col_l.at[pl.ds(row, ROWS)], at(1, dt))
+
+    near = ((1, HALO - NEAR), (-1, HALO + ROWS))
+    far = ((2, 0), (-2, HALO + ROWS + NEAR))
+    last = ext.at[SOUTH, HALO + ROWS - 1]
+    send(last.at[:, pl.ds(0, 128)], sx_r, at(-1, 2))
+    send(last.at[:, pl.ds(COLS - 128, 128)], sx_l, at(1, 2))
+    send(last.at[:, pl.ds(0, COLS)], sx, at(0, 2))
+    for dt, row in near:
+        send_columns(dt, row)
+    for dt, row in near:
+        send_rows(0, EARLY, dt, row)
+    send_columns(0, HALO)
     first = len(halo)
-    send_fields(EARLY, 1)
-    for c in halo[:first]:
+    for c in halo:
         c.wait_recv()
+    for dt, row in far:
+        send_rows(0, LATE, dt, row)
+        send_columns(dt, row)
+    second = len(halo)
+    for dt, row in near + ((0, HALO),):
+        if dt:
+            send_rows(EARLY, 1, dt, row)
+        send(ext.at[EARLY, own, :, pl.ds(0, 128)], early_r.at[pl.ds(row, ROWS)], at(-1, dt))
+        send(
+            ext.at[EARLY, own, :, pl.ds(COLS - 128, 128)], early_l.at[pl.ds(row, ROWS)], at(1, dt)
+        )
     pl.semaphore_wait(reach.at[0], 2)
     for dz in (-4, 4):
         pl.semaphore_signal(reach.at[1], inc=1, device_id=at(0, 4 * dz), device_id_type=MESH)
 
-    right = lax.broadcasted_iota(jnp.int32, (LAYERS, 128), 1) < 64
-    def merge_columns(f):
-        for r in range(SPAN):
-            ext[f, r, :, COLS:] = jnp.where(right, col_r[f, r], col_l[f, r])
-
-    for f in range(EARLY):
-        merge_columns(f)
-    north = jnp.concatenate([sx[...], jnp.where(right, sx_r[...], sx_l[...])], axis=1)
-    for r in range(SPAN):
-        east = ext[EAST, r]
-        west = prev_col(east)
-        south = ext[SOUTH, r]
-        upward = ext[UP, r]
-        downward = prev_layer(upward)
-        d = ext[CAP, r] + east + west + south + north + upward + downward
-        inv = 1.0 / d
-        diag[0, r] = d
-        diag[1, r] = inv
-        g[0, r] = ext[LATE, r] * inv
-        for i, c in enumerate((east, west, south, north, upward, downward)):
-            coef[i, r] = c * inv
-        north = south
+    slot = lax.broadcasted_iota(jnp.int32, (LAYERS, 128), 1)
+
+    def merge_columns(fields, rows):
+        for r in rows:
+            to_right, to_left = col_r[r], col_l[r]
+            for f in range(fields):
+                a = pltpu.roll(to_right, (128 - EDGE * f) % 128, 1)
+                b = pltpu.roll(to_left, (256 - EDGE * (f + 1)) % 128, 1)
+                rest = jnp.where(slot >= 128 - EDGE, b, 1.0 if f == CAP else 0.0)
+                ext[f, r, :, COLS:] = jnp.where(slot < EDGE, a, rest)
+
+    def make_couplings(rows, north, diagonals):
+        for r in rows:
+            east = ext[EAST, r]
+            west = prev_col(east)
+            south = ext[SOUTH, r]
+            upward = ext[UP, r]
+            downward = prev_layer(upward)
+            d = ext[CAP, r] + east + west + south + north + upward + downward
+            inv = 1.0 / d
+            if diagonals:
+                diag[0, r] = d
+                diag[1, r] = inv
+                g[0, r] = ext[LATE, r] * inv
+            for i, c in enumerate((east, west, south, north, upward, downward)):
+                coef[i, r] = c * inv
+            north = south
+
+    rows_near = range(HALO - NEAR, HALO + ROWS + NEAR)
+    merge_columns(EARLY, rows_near)
+    above = jnp.concatenate([sx[...], jnp.where(slot < 64, sx_r[...], sx_l[...])], axis=1)
+    make_couplings(rows_near, above, True)
+
+    def far_couplings():
+        for c in halo[first:second]:
+            c.wait_recv()
+        end = HALO + ROWS + NEAR
+        for rows in (range(0, HALO - NEAR), range(end, SPAN)):
+            merge_columns(LATE, rows)
+        make_couplings(range(1, HALO - NEAR), ext[SOUTH, 0], False)
+        make_couplings(range(end, SPAN - 1), ext[SOUTH, end - 1], False)
 
     (q1, p1), (q2, p2), (q3, p3) = sweep_constants()
 
-    def smooth(gi, ui):
-        for r in range(1, SPAN - 1):
+    def smooth(gi, ui, lo, hi):
+        for r in range(lo + 1, hi - 1):
             z1[r] = ((1.0 + q1 - p1) / centre + p1) * gi[r] + (p1 / centre) * neighbours(gi, coef, r)
-        for r in range(2, SPAN - 2):
+        for r in range(lo + 2, hi - 2):
             z2[r] = (1.0 + q2 - p2) * z1[r] + (p2 - q2 / centre) * gi[r] + p2 * neighbours(z1, coef, r)
-        for r in range(3, SPAN - 3):
+        for r in range(lo + 3, hi - 3):
             ui[r] = (
                 (1.0 + q3 - p3) * z2[r] - q3 * z1[r] + p3 * gi[r] + p3 * neighbours(z2, coef, r)
             )
 
-    def rows_both_ways(ref, above, below, ssem, rsem):
+    pending = []
+
+    def send_all(src, targets, ssem, rsem):
         copies = []
-        for n, (dt, dst) in enumerate(((1, above), (-1, below))):
+        for n, (dt, dst) in enumerate(targets):
             c = pltpu.make_async_remote_copy(
-                src_ref=ref.at[own], dst_ref=dst,
-                send_sem=ssem.at[n], recv_sem=rsem.at[n], device_id=at(0, dt), device_id_type=MESH,
+                src_ref=src, dst_ref=dst, send_sem=ssem.at[n], recv_sem=rsem.at[n],
+                device_id=at(0, dt), device_id_type=MESH,
             )
             c.start()
             copies.append(c)
+        pending.extend(copies)
         return copies
 
-    pending = []
-
-    def chain(base):
+    def send_u(i, n):
+        return send_all(
+            u.at[i, own], ((1, uh.at[n, pl.ds(0, NEAR)]), (-1, uh.at[n, pl.ds(NEAR, NEAR)])),
+            ush_send.at[n], ush_recv.at[n],
+        )
+
+    def chain(base, beside):
         parts = [None] * 6
-        for i in range(3):
+        spans = ((HALO - NEAR, HALO + ROWS + NEAR), (0, SPAN), (HALO - NEAR, HALO + ROWS + NEAR))
+        for i, (lo, hi) in enumerate(spans):
             gi, ui = g.at[base + i], u.at[base + i]
-            smooth(gi, ui)
             gn = g.at[base + i + 1] if i < 2 else z1
-            for r in range(HALO, HALO + ROWS):
+            smooth(gi, ui, lo, hi)
+            for r in range(lo + 4, hi - 4):
                 gn[r] = gi[r] - ui[r] + neighbours(ui, coef, r)
-            if i < 2:
-                k = base // 3 * 2 + i
-                copies = rows_both_ways(
-                    gn, gn.at[pl.ds(0, HALO)], gn.at[pl.ds(HALO + ROWS, HALO)],
+            if i == 0:
+                k = base // 3
+                copies = send_all(
+                    gn.at[own],
+                    [(dt, gn.at[pl.ds(row, ROWS)]) for dt, row in far + near],
                     mid_send.at[k], mid_recv.at[k],
                 )
-                pending.extend(copies)
+                beside()
             for r in range(HALO, HALO + ROWS):
                 du = (diag[0, r] * ui[r])[:, :COLS]
                 for k, ref in ((2 * i, gi), (2 * i + 1, gn)):
                     term = du * ref[r][:, :COLS]
                     parts[k] = term if parts[k] is None else parts[k] + term
-            if i < 2:
+            if i == 0:
                 for c in copies:
                     c.wait_recv()
         lanes = lax.broadcasted_iota(jnp.int32, (1, 128), 1)
@@ -312,28 +368,33 @@
         ]
         return krylov_coefficients(mu)
 
-    a0[core] = chain(0).reshape(1, 1, 128)
-    for i in range(3):
-        copies = rows_both_ways(
-            u.at[i], uh.at[i, pl.ds(0, HALO)], uh.at[i, pl.ds(HALO, HALO)],
-            ush_send.at[i], ush_recv.at[i],
-        )
-        pending.extend(copies)
-    shadow = pending[-6:]
-    for c in halo[first:]:
+    shadow = []
+
+    def beside():
+        shadow.extend(send_u(0, 0))
+        far_couplings()
+
+    a0[core] = chain(0, beside).reshape(1, 1, 128)
+    shadow.extend(send_u(2, 1))
+    for c in halo[second:]:
         c.wait_recv()
-    merge_columns(EARLY)
-    pl.semaphore_wait(reach.at[1], 2)
+    for r in rows_near:
+        ext[EARLY, r, :, COLS:] = jnp.where(slot < 64, early_r[r], early_l[r])
     for c in loads[8:10]:
         c.wait()
+    pl.semaphore_wait(reach.at[1], 2)
     c1 = coefficients(all_sum((a0, a1, a2), 0).reshape(1, 128))
     for c in shadow:
         c.wait_recv()
     held = jnp.zeros((LAYERS, COLS), jnp.float32)
-    for r in range(SPAN):
+    for r in rows_near:
         inside = HALO <= r < HALO + ROWS
-        src, s = (u, r) if inside else (uh, r if r < HALO else r - ROWS)
-        v = c1[0] * src[0, s] + c1[1] * src[1, s] + c1[2] * src[2, s]
+        if inside:
+            ends = u[0, r], u[2, r]
+        else:
+            n = r - (HALO - NEAR) if r < HALO else r - HALO
+            ends = uh[0, n], uh[1, n]
+        v = c1[0] * ends[0] + c1[1] * u[1, r] + c1[2] * ends[1]
         g[3, r] = (ext[EARLY, r] + ext[CAP, r] * v) * diag[1, r]
         if inside:
             out_late[:, r - HALO, :] = v[:, :COLS]
@@ -349,7 +410,7 @@
 
     for c in loads[10:]:
         c.wait()
-    moments = chain(3)
+    moments = chain(3, lambda: None)
     terms = [held]
     for i in range(3):
         t = None
@@ -401,14 +462,21 @@
         c.wait()
 
 
-def finish(late, early, bank, out_late, out_early, out_bank, sem):
-    copies = [
+def finish(late, early, bank, out_late, out_early, out_bank, late_v, early_v, bank_v, sem):
+    ins = [
         pltpu.make_async_copy(src, dst, sem.at[n])
-        for n, (src, dst) in enumerate(((late, out_late), (early, out_early), (bank, out_bank)))
+        for n, (src, dst) in enumerate(((late, late_v), (early, early_v), (bank, bank_v)))
     ]
-    for c in copies:
+    outs = [
+        pltpu.make_async_copy(src, dst, sem.at[3 + n])
+        for n, (src, dst) in enumerate(((late_v, out_late), (early_v, out_early), (bank_v, out_bank)))
+    ]
+    for c in ins:
         c.start()
-    for c in copies:
+    for c, d in zip(ins, outs):
+        c.wait()
+        d.start()
+    for c in outs:
         c.wait()
 
 
@@ -436,8 +504,12 @@
             pltpu.VMEM((LAYERS, 16), i32),
             field, field, field, field,
             pltpu.VMEM((FIELDS,) + wide, f32),
-            pltpu.VMEM((FIELDS, SPAN, LAYERS, 128), f32),
-            pltpu.VMEM((FIELDS, SPAN, LAYERS, 128), f32),
+            pltpu.VMEM((ROWS, LAYERS, 128), f32),
+            pltpu.VMEM((ROWS, LAYERS, 128), f32),
+            pltpu.VMEM((SPAN, LAYERS, 128), f32),
+            pltpu.VMEM((SPAN, LAYERS, 128), f32),
+            pltpu.VMEM((SPAN, LAYERS, 128), f32),
+            pltpu.VMEM((SPAN, LAYERS, 128), f32),
             pltpu.VMEM((LAYERS, COLS), f32),
             pltpu.VMEM((LAYERS, 128), f32),
             pltpu.VMEM((LAYERS, 128), f32),
@@ -445,7 +517,7 @@
             pltpu.VMEM((2,) + wide, f32),
             pltpu.VMEM((6,) + wide, f32),
             pltpu.VMEM((6,) + wide, f32),
-            pltpu.VMEM((3, 2 * HALO, LAYERS, WIDE), f32),
+            pltpu.VMEM((2, 2 * NEAR, LAYERS, WIDE), f32),
             pltpu.VMEM(wide, f32),
             pltpu.VMEM(wide, f32),
             pltpu.VMEM((2, 1, 1, 128), f32),
@@ -456,12 +528,12 @@
             pltpu.VMEM((16, 9, 1, 128), f32),
             dma((11,)),
             dma((3,)),
-            dma((19,)),
-            dma((19,)),
-            dma((4, 2)),
-            dma((4, 2)),
-            dma((3, 2)),
-            dma((3, 2)),
+            dma((25,)),
+            dma((25,)),
+            dma((2, 4)),
+            dma((2, 4)),
+            dma((2, 2)),
+            dma((2, 2)),
             dma((6,)),
             dma((6,)),
             pltpu.SemaphoreType.REGULAR((2,)),
@@ -479,7 +551,7 @@
         out_shape=shapes,
         in_specs=[hbm] * 3,
         out_specs=(hbm,) * 3,
-        scratch_shapes=[dma((3,))],
+        scratch_shapes=[field, field, pltpu.VMEM((1, BANKS), f32), dma((6,))],
         compiler_params=pltpu.CompilerParams(vmem_limit_bytes=60 << 20),
         name="write_results",
     )(*results)

time: 76.5 us -> 72.4 us (0.946)
  Pallas kernels: 75.6 us -> 71.5 us
    pallas_call x1, Pallas kernels: 72.5 us -> 70 us  [on_device(): pl.pallas_call(kernel, out_shape=shapes, in_specs=[hbm] * 11, out_specs=(...]
    pallas_call x1, Pallas kernels: 3.15 us -> 1.44 us  [on_device(): pl.pallas_call(finish, out_shape=shapes, in_specs=[hbm] * 3, out_specs=(h...]
where the time goes in v3:
time: 72.4 us; the launch traced here: 72.1 us
  Pallas kernels  71.5 us (99%)
    pallas_call x1, Pallas kernels, on_device(): pl.pallas_call(kernel, out_shape=shapes, in_specs=[hbm] * 11, out_specs=(...  70 us

profile of v3, /device:TPU:1, one launch (start us, length us, event | category | flops | bytes accessed | tf_op | source)
XLA Modules:
  0.0 72.1 jit_solution(5121207375333960980)
XLA Ops:
  0.6 70.0 %adjoint_steps.1 = (f32[8,4,256]{2,1,0:T(4,128)}, f32[8,4,256]{2,1,0:T(4,128)}, f32[1,256]{1,0:T(1,128)}) custom-call(f32[8,4,256]{2,1,0:T(4,128)} %cond_x_in.1, f32[8,4,256]{2,1,0:T(4,128)} %cond_y_in.1, f32[8,4,256]{2,1,0:T(4,128)} %via_in.1, f32[8,4,256]{2,1,0:T(4,128)} %cap_in.1, s32[4,256]{1,0:T(4,128)} %cls_in.1, s32[8,8]{1,0:T(8,128)} %mask_in.1, ...), custom_call_target="tpu_custom_call" | custom-call | tf_op jit(solution)/shard_map/adjoint_steps/pallas_call | solution.py:494
  70.7 1.4 %write_results.1 = (f32[8,4,256]{2,1,0:T(4,128)}, f32[8,4,256]{2,1,0:T(4,128)}, f32[1,256]{1,0:T(1,128)}) custom-call(f32[8,4,256]{2,1,0:T(4,128)} %get-tuple-element.9.late, f32[8,4,256]{2,1,0:T(4,128)} %get-tuple-element.10.early, f32[1,256]{1,0:T(1,128)} %get-tuple-element.11.bank), custom_call_target="tpu_custom_call" | custom-call | tf_op jit(solution)/shard_map/write_results/pallas_call | solution.py:549

commit v4 on v3

--- a/solution.py
+++ b/solution.py
@@ -14,8 +14,7 @@
 LAYERS = 8
 ROWS = 4
 COLS = 256
-HALO = 8
-NEAR = 4
+HALO = 4
 SPAN = ROWS + 2 * HALO
 WIDE = COLS + 128
 EDGE = 24
@@ -100,7 +99,7 @@
     cond_x_in, cond_y_in, via_in, cap_in, cls_in, mask_in, bank_in, late_in, early_in, rate_late_in, rate_early_in,
     late_out, early_out, bank_out,
     out_late, out_early, out_bank, cond_x, cond_y, via, cap, cls, mask, bank, late, early, rate_late, rate_early,
-    ext, pack_r, pack_l, col_r, col_l, early_r, early_l, sx, sx_r, sx_l, coef, diag, g, u, uh, z1, z2,
+    ext, pack_r, pack_l, col_r, col_l, early_r, early_l, sx, sx_r, sx_l, coef, diag, g, u, uh, pg, pu, pn, z1, z2,
     a0, a1, a2, b0, b1, b2,
     load_sem, store_sem, halo_send, halo_recv, mid_send, mid_recv, ush_send, ush_recv, sum_send, sum_recv, reach,
 ):
@@ -203,8 +202,7 @@
         send(pack_r, col_r.at[pl.ds(row, ROWS)], at(-1, dt))
         send(pack_l, col_l.at[pl.ds(row, ROWS)], at(1, dt))
 
-    near = ((1, HALO - NEAR), (-1, HALO + ROWS))
-    far = ((2, 0), (-2, HALO + ROWS + NEAR))
+    near = ((1, 0), (-1, HALO + ROWS))
     last = ext.at[SOUTH, HALO + ROWS - 1]
     send(last.at[:, pl.ds(0, 128)], sx_r, at(-1, 2))
     send(last.at[:, pl.ds(COLS - 128, 128)], sx_l, at(1, 2))
@@ -217,10 +215,6 @@
     first = len(halo)
     for c in halo:
         c.wait_recv()
-    for dt, row in far:
-        send_rows(0, LATE, dt, row)
-        send_columns(dt, row)
-    second = len(halo)
     for dt, row in near + ((0, HALO),):
         if dt:
             send_rows(EARLY, 1, dt, row)
@@ -234,65 +228,51 @@
 
     slot = lax.broadcasted_iota(jnp.int32, (LAYERS, 128), 1)
 
-    def merge_columns(fields, rows):
-        for r in rows:
-            to_right, to_left = col_r[r], col_l[r]
-            for f in range(fields):
-                a = pltpu.roll(to_right, (128 - EDGE * f) % 128, 1)
-                b = pltpu.roll(to_left, (256 - EDGE * (f + 1)) % 128, 1)
-                rest = jnp.where(slot >= 128 - EDGE, b, 1.0 if f == CAP else 0.0)
-                ext[f, r, :, COLS:] = jnp.where(slot < EDGE, a, rest)
-
-    def make_couplings(rows, north, diagonals):
-        for r in rows:
-            east = ext[EAST, r]
-            west = prev_col(east)
-            south = ext[SOUTH, r]
-            upward = ext[UP, r]
-            downward = prev_layer(upward)
-            d = ext[CAP, r] + east + west + south + north + upward + downward
-            inv = 1.0 / d
-            if diagonals:
-                diag[0, r] = d
-                diag[1, r] = inv
-                g[0, r] = ext[LATE, r] * inv
-            for i, c in enumerate((east, west, south, north, upward, downward)):
-                coef[i, r] = c * inv
-            north = south
-
-    rows_near = range(HALO - NEAR, HALO + ROWS + NEAR)
-    merge_columns(EARLY, rows_near)
-    above = jnp.concatenate([sx[...], jnp.where(slot < 64, sx_r[...], sx_l[...])], axis=1)
-    make_couplings(rows_near, above, True)
-
-    def far_couplings():
-        for c in halo[first:second]:
-            c.wait_recv()
-        end = HALO + ROWS + NEAR
-        for rows in (range(0, HALO - NEAR), range(end, SPAN)):
-            merge_columns(LATE, rows)
-        make_couplings(range(1, HALO - NEAR), ext[SOUTH, 0], False)
-        make_couplings(range(end, SPAN - 1), ext[SOUTH, end - 1], False)
+    for r in range(SPAN):
+        to_right, to_left = col_r[r], col_l[r]
+        for f in range(EARLY):
+            a = pltpu.roll(to_right, (128 - EDGE * f) % 128, 1)
+            b = pltpu.roll(to_left, (256 - EDGE * (f + 1)) % 128, 1)
+            rest = jnp.where(slot >= 128 - EDGE, b, 1.0 if f == CAP else 0.0)
+            ext[f, r, :, COLS:] = jnp.where(slot < EDGE, a, rest)
+    north = jnp.concatenate([sx[...], jnp.where(slot < 64, sx_r[...], sx_l[...])], axis=1)
+    for r in range(SPAN):
+        east = ext[EAST, r]
+        west = prev_col(east)
+        south = ext[SOUTH, r]
+        upward = ext[UP, r]
+        downward = prev_layer(upward)
+        d = ext[CAP, r] + east + west + south + north + upward + downward
+        inv = 1.0 / d
+        diag[0, r] = d
+        diag[1, r] = inv
+        g[0, r] = ext[LATE, r] * inv
+        for i, c in enumerate((east, west, south, north, upward, downward)):
+            coef[i, r] = c * inv
+        north = south
 
     (q1, p1), (q2, p2), (q3, p3) = sweep_constants()
 
-    def smooth(gi, ui, lo, hi):
-        for r in range(lo + 1, hi - 1):
+    def iterate(gi, ui, gn):
+        for r in range(1, SPAN - 1):
             z1[r] = ((1.0 + q1 - p1) / centre + p1) * gi[r] + (p1 / centre) * neighbours(gi, coef, r)
-        for r in range(lo + 2, hi - 2):
+        for r in range(2, SPAN - 2):
             z2[r] = (1.0 + q2 - p2) * z1[r] + (p2 - q2 / centre) * gi[r] + p2 * neighbours(z1, coef, r)
-        for r in range(lo + 3, hi - 3):
+        for r in range(3, SPAN - 3):
             ui[r] = (
                 (1.0 + q3 - p3) * z2[r] - q3 * z1[r] + p3 * gi[r] + p3 * neighbours(z2, coef, r)
             )
-
+        for r in own_rows:
+            gn[r] = gi[r] - ui[r] + neighbours(ui, coef, r)
+
+    own_rows = range(HALO, HALO + ROWS)
     pending = []
 
-    def send_all(src, targets, ssem, rsem):
+    def send_block(src, above, below, ssem, rsem):
         copies = []
-        for n, (dt, dst) in enumerate(targets):
+        for n, (dt, dst) in enumerate(((1, above), (-1, below))):
             c = pltpu.make_async_remote_copy(
-                src_ref=src, dst_ref=dst, send_sem=ssem.at[n], recv_sem=rsem.at[n],
+                src_ref=src.at[own], dst_ref=dst, send_sem=ssem.at[n], recv_sem=rsem.at[n],
                 device_id=at(0, dt), device_id_type=MESH,
             )
             c.start()
@@ -300,44 +280,36 @@
         pending.extend(copies)
         return copies
 
-    def send_u(i, n):
-        return send_all(
-            u.at[i, own], ((1, uh.at[n, pl.ds(0, NEAR)]), (-1, uh.at[n, pl.ds(NEAR, NEAR)])),
-            ush_send.at[n], ush_recv.at[n],
-        )
-
-    def chain(base, beside):
-        parts = [None] * 6
-        spans = ((HALO - NEAR, HALO + ROWS + NEAR), (0, SPAN), (HALO - NEAR, HALO + ROWS + NEAR))
-        for i, (lo, hi) in enumerate(spans):
-            gi, ui = g.at[base + i], u.at[base + i]
-            gn = g.at[base + i + 1] if i < 2 else z1
-            smooth(gi, ui, lo, hi)
-            for r in range(lo + 4, hi - 4):
-                gn[r] = gi[r] - ui[r] + neighbours(ui, coef, r)
-            if i == 0:
-                k = base // 3
-                copies = send_all(
-                    gn.at[own],
-                    [(dt, gn.at[pl.ds(row, ROWS)]) for dt, row in far + near],
-                    mid_send.at[k], mid_recv.at[k],
-                )
-                beside()
-            for r in range(HALO, HALO + ROWS):
-                du = (diag[0, r] * ui[r])[:, :COLS]
-                for k, ref in ((2 * i, gi), (2 * i + 1, gn)):
-                    term = du * ref[r][:, :COLS]
-                    parts[k] = term if parts[k] is None else parts[k] + term
-            if i == 0:
-                for c in copies:
-                    c.wait_recv()
+    def send_g(ref, n):
+        return send_block(
+            ref, ref.at[pl.ds(0, HALO)], ref.at[pl.ds(HALO + ROWS, HALO)], mid_send.at[n], mid_recv.at[n]
+        )
+
+    def send_u(i):
+        return send_block(
+            u.at[i], uh.at[i, pl.ds(0, HALO)], uh.at[i, pl.ds(HALO, HALO)],
+            ush_send.at[i], ush_recv.at[i],
+        )
+
+    def arrive(copies):
+        for c in copies:
+            c.wait_recv()
+
+    def add_products(parts, i, gi, ui, gn):
+        for r in own_rows:
+            du = (diag[0, r] * ui[r])[:, :COLS]
+            for k, ref in ((2 * i, gi), (2 * i + 1, gn)):
+                term = du * ref[r][:, :COLS]
+                parts[k] = term if parts[k] is None else parts[k] + term
+
+    def moment_row(parts):
         lanes = lax.broadcasted_iota(jnp.int32, (1, 128), 1)
         row = jnp.zeros((1, 128), jnp.float32)
         for k, p in enumerate(parts):
             row = jnp.where(lanes == k, jnp.sum(p, axis=(0, 1), keepdims=True), row)
         return row
 
-    def group_sum(buf, me, peers, n, ssem, rsem):
+    def group_sum(buf, me, peers, n, ssem, rsem, beside=None):
         for d in peers:
             pltpu.make_async_remote_copy(
                 src_ref=buf.at[me], dst_ref=buf.at[me], send_sem=ssem, recv_sem=rsem,
@@ -348,6 +320,8 @@
             src_ref=most, dst_ref=most, send_sem=ssem, recv_sem=rsem,
             device_id=peers[0], device_id_type=MESH,
         )
+        if beside is not None:
+            beside()
         whole.wait_recv()
         pending.append(whole)
         total = buf[0]
@@ -355,11 +329,13 @@
             total = total + buf[i]
         return total
 
-    def all_sum(bufs, base):
+    def all_sum(bufs, base, beside=(None, None, None)):
         c, p, w = bufs
-        p[y * 4 + x] = group_sum(c, core, core_peer, 2, sum_send.at[base], sum_recv.at[base])
-        w[z] = group_sum(p, y * 4 + x, plane_peers, 16, sum_send.at[base + 1], sum_recv.at[base + 1])
-        return group_sum(w, z, z_peers, 16, sum_send.at[base + 2], sum_recv.at[base + 2])
+        xy = y * 4 + x
+        send, recv = sum_send.at, sum_recv.at
+        p[xy] = group_sum(c, core, core_peer, 2, send[base], recv[base], beside[0])
+        w[z] = group_sum(p, xy, plane_peers, 16, send[base + 1], recv[base + 1], beside[1])
+        return group_sum(w, z, z_peers, 16, send[base + 2], recv[base + 2], beside[2])
 
     def coefficients(row):
         lanes = lax.broadcasted_iota(jnp.int32, (1, 128), 1)
@@ -368,38 +344,65 @@
         ]
         return krylov_coefficients(mu)
 
-    shadow = []
-
-    def beside():
-        shadow.extend(send_u(0, 0))
-        far_couplings()
-
-    a0[core] = chain(0, beside).reshape(1, 1, 128)
-    shadow.extend(send_u(2, 1))
-    for c in halo[second:]:
-        c.wait_recv()
-    for r in rows_near:
-        ext[EARLY, r, :, COLS:] = jnp.where(slot < 64, early_r[r], early_l[r])
+    parts = [None] * 6
+    iterate(g.at[0], u.at[0], g.at[1])
+    moving = send_g(g.at[1], 0)
+    shared = [send_u(0)]
+    add_products(parts, 0, g.at[0], u.at[0], g.at[1])
+    arrive(moving)
+    iterate(g.at[1], u.at[1], g.at[2])
+    moving = send_g(g.at[2], 1)
+    shared.append(send_u(1))
+    add_products(parts, 1, g.at[1], u.at[1], g.at[2])
+    traded = []
+
+    def source_part():
+        arrive(halo[first:])
+        for r in range(SPAN):
+            ext[EARLY, r, :, COLS:] = jnp.where(slot < 64, early_r[r], early_l[r])
+            pg[0, r] = ext[EARLY, r] * diag[1, r]
+        iterate(pg.at[0], pu.at[0], pn.at[0])
+        traded.extend(send_g(pn.at[0], 2))
+
+    def field_part(i):
+        arrive(shared[i])
+        for r in range(SPAN):
+            if r in own_rows:
+                v = u[i, r]
+            else:
+                v = uh[i, r if r < HALO else r - ROWS]
+            pg[1 + i, r] = ext[CAP, r] * diag[1, r] * v
+        iterate(pg.at[1 + i], pu.at[1 + i], pn.at[1 + i])
+        traded.extend(send_g(pn.at[1 + i], 3 + i))
+
+    source_part()
+    field_part(0)
+    arrive(moving)
+    iterate(g.at[2], u.at[2], z1)
+    add_products(parts, 2, g.at[2], u.at[2], z1)
+    a0[core] = moment_row(parts).reshape(1, 1, 128)
     for c in loads[8:10]:
         c.wait()
     pl.semaphore_wait(reach.at[1], 2)
-    c1 = coefficients(all_sum((a0, a1, a2), 0).reshape(1, 128))
-    for c in shadow:
-        c.wait_recv()
+    row = all_sum(
+        (a0, a1, a2), 0,
+        (lambda: shared.append(send_u(2)), lambda: field_part(1), lambda: field_part(2)),
+    )
+    c1 = coefficients(row.reshape(1, 128))
+    arrive(traded)
     held = jnp.zeros((LAYERS, COLS), jnp.float32)
-    for r in rows_near:
-        inside = HALO <= r < HALO + ROWS
-        if inside:
-            ends = u[0, r], u[2, r]
-        else:
-            n = r - (HALO - NEAR) if r < HALO else r - HALO
-            ends = uh[0, n], uh[1, n]
-        v = c1[0] * ends[0] + c1[1] * u[1, r] + c1[2] * ends[1]
-        g[3, r] = (ext[EARLY, r] + ext[CAP, r] * v) * diag[1, r]
-        if inside:
-            out_late[:, r - HALO, :] = v[:, :COLS]
-            held = held + v[:, :COLS] * rate_late[:, r - HALO, :]
-
+    for r in range(SPAN):
+        g[3, r] = pn[0, r] + c1[0] * pn[1, r] + c1[1] * pn[2, r] + c1[2] * pn[3, r]
+        if r in own_rows:
+            g[5, r] = pg[0, r] + c1[0] * pg[1, r] + c1[1] * pg[2, r] + c1[2] * pg[3, r]
+            u[5, r] = pu[0, r] + c1[0] * pu[1, r] + c1[1] * pu[2, r] + c1[2] * pu[3, r]
+    parts = [None] * 6
+    iterate(g.at[3], u.at[3], g.at[4])
+    moving = send_g(g.at[4], 6)
+    for r in own_rows:
+        v = c1[0] * u[0, r] + c1[1] * u[1, r] + c1[2] * u[2, r]
+        out_late[:, r - HALO, :] = v[:, :COLS]
+        held = held + v[:, :COLS] * rate_late[:, r - HALO, :]
     stores = [
         pltpu.make_async_copy(src, dst, store_sem.at[n])
         for n, (src, dst) in enumerate(
@@ -408,14 +411,19 @@
     ]
     stores[0].start()
 
+    add_products(parts, 0, g.at[5], u.at[5], g.at[3])
+    add_products(parts, 1, g.at[3], u.at[3], g.at[4])
     for c in loads[10:]:
         c.wait()
-    moments = chain(3, lambda: None)
+    arrive(moving)
+    iterate(g.at[4], u.at[4], z1)
+    add_products(parts, 2, g.at[4], u.at[4], z1)
+    moments = moment_row(parts)
     terms = [held]
-    for i in range(3):
+    for i in (5, 3, 4):
         t = None
-        for r in range(ROWS):
-            w = u[3 + i, HALO + r][:, :COLS] * rate_early[:, r, :]
+        for r in own_rows:
+            w = u[i, r][:, :COLS] * rate_early[:, r - HALO, :]
             t = w if t is None else t + w
         terms.append(t)
 
@@ -450,7 +458,7 @@
         )
     for r in range(ROWS):
         e = HALO + r
-        v = c2[0] * u[3, e] + c2[1] * u[4, e] + c2[2] * u[5, e]
+        v = c2[0] * u[5, e] + c2[1] * u[3, e] + c2[2] * u[4, e]
         out_early[:, r, :] = v[:, :COLS]
     stores[1].start()
     stores[2].start()
@@ -517,7 +525,10 @@
             pltpu.VMEM((2,) + wide, f32),
             pltpu.VMEM((6,) + wide, f32),
             pltpu.VMEM((6,) + wide, f32),
-            pltpu.VMEM((2, 2 * NEAR, LAYERS, WIDE), f32),
+            pltpu.VMEM((3, 2 * HALO, LAYERS, WIDE), f32),
+            pltpu.VMEM((4,) + wide, f32),
+            pltpu.VMEM((4,) + wide, f32),
+            pltpu.VMEM((4,) + wide, f32),
             pltpu.VMEM(wide, f32),
             pltpu.VMEM(wide, f32),
             pltpu.VMEM((2, 1, 1, 128), f32),
@@ -528,12 +539,12 @@
             pltpu.VMEM((16, 9, 1, 128), f32),
             dma((11,)),
             dma((3,)),
-            dma((25,)),
-            dma((25,)),
-            dma((2, 4)),
-            dma((2, 4)),
-            dma((2, 2)),
-            dma((2, 2)),
+            dma((19,)),
+            dma((19,)),
+            dma((7, 2)),
+            dma((7, 2)),
+            dma((3, 2)),
+            dma((3, 2)),
             dma((6,)),
             dma((6,)),
             pltpu.SemaphoreType.REGULAR((2,)),

time: 72.4 us -> 66.7 us (0.921)
  Pallas kernels: 71.5 us -> 65.6 us
    pallas_call x1, Pallas kernels: 70 us -> 64.2 us  [on_device(): pl.pallas_call(kernel, out_shape=shapes, in_specs=[hbm] * 11, out_specs=(...]
where the time goes in v4:
time: 66.7 us; the launch traced here: 66.3 us
  Pallas kernels  65.6 us (98%)
    pallas_call x1, Pallas kernels, on_device(): pl.pallas_call(kernel, out_shape=shapes, in_specs=[hbm] * 11, out_specs=(...  64.2 us
    pallas_call x1, Pallas kernels, on_device(): pl.pallas_call(finish, out_shape=shapes, in_specs=[hbm] * 3, out_specs=(h...  1.44 us

profile of v4, /device:TPU:1, one launch (start us, length us, event | category | flops | bytes accessed | tf_op | source)
XLA Modules:
  0.0 66.3 jit_solution(13179745319497937236)
XLA Ops:
  0.6 64.2 %adjoint_steps.1 = (f32[8,4,256]{2,1,0:T(4,128)}, f32[8,4,256]{2,1,0:T(4,128)}, f32[1,256]{1,0:T(1,128)}) custom-call(f32[8,4,256]{2,1,0:T(4,128)} %cond_x_in.1, f32[8,4,256]{2,1,0:T(4,128)} %cond_y_in.1, f32[8,4,256]{2,1,0:T(4,128)} %via_in.1, f32[8,4,256]{2,1,0:T(4,128)} %cap_in.1, s32[4,256]{1,0:T(4,128)} %cls_in.1, s32[8,8]{1,0:T(8,128)} %mask_in.1, ...), custom_call_target="tpu_custom_call" | custom-call | tf_op jit(solution)/shard_map/adjoint_steps/pallas_call | solution.py:502
  64.8 1.4 %write_results.1 = (f32[8,4,256]{2,1,0:T(4,128)}, f32[8,4,256]{2,1,0:T(4,128)}, f32[1,256]{1,0:T(1,128)}) custom-call(f32[8,4,256]{2,1,0:T(4,128)} %get-tuple-element.9.late, f32[8,4,256]{2,1,0:T(4,128)} %get-tuple-element.10.early, f32[1,256]{1,0:T(1,128)} %get-tuple-element.11.bank), custom_call_target="tpu_custom_call" | custom-call | tf_op jit(solution)/shard_map/write_results/pallas_call | solution.py:560

commit v5 on v4

--- a/solution.py
+++ b/solution.py
@@ -99,8 +99,8 @@
     cond_x_in, cond_y_in, via_in, cap_in, cls_in, mask_in, bank_in, late_in, early_in, rate_late_in, rate_early_in,
     late_out, early_out, bank_out,
     out_late, out_early, out_bank, cond_x, cond_y, via, cap, cls, mask, bank, late, early, rate_late, rate_early,
-    ext, pack_r, pack_l, col_r, col_l, early_r, early_l, sx, sx_r, sx_l, coef, diag, g, u, uh, pg, pu, pn, z1, z2,
-    a0, a1, a2, b0, b1, b2,
+    ext, pack_r, pack_l, col_r, col_l, early_r, early_l, sx, sx_r, sx_l, coef, diag, g, u, uh, pg, pu, z1, z2,
+    a0, a1, a2, b0, b1, b2, b3,
     load_sem, store_sem, halo_send, halo_recv, mid_send, mid_recv, ush_send, ush_recv, sum_send, sum_recv, reach,
 ):
     loads = [
@@ -121,8 +121,14 @@
     y, core = lay // 2, lay % 2
     z, x = til // 4, til % 4
 
+    around = {
+        (dl, dt): ((lay + dl + lays) % lays, (til + dt + tils) % tils)
+        for dt in (-16, -8, -4, -2, -1, 0, 1, 2, 4, 8, 16)
+        for dl in ((-1, 0, 1) if -2 <= dt <= 2 else (0,))
+    }
+
     def at(dl, dt):
-        return ((lay + dl + lays) % lays, (til + dt + tils) % tils)
+        return around[dl, dt]
 
     core_peer = [(lay + 1 - 2 * core, til)]
     plane_peers = [
@@ -354,15 +360,20 @@
     moving = send_g(g.at[2], 1)
     shared.append(send_u(1))
     add_products(parts, 1, g.at[1], u.at[1], g.at[2])
-    traded = []
+    traded = {}
+
+    def part_step(step, n):
+        if step:
+            arrive(traded[0, n])
+        iterate(pg.at[step, n], pu.at[step, n], pg.at[step + 1, n])
+        traded[step, n] = send_g(pg.at[step + 1, n], 2 + 4 * step + n)
 
     def source_part():
         arrive(halo[first:])
         for r in range(SPAN):
             ext[EARLY, r, :, COLS:] = jnp.where(slot < 64, early_r[r], early_l[r])
-            pg[0, r] = ext[EARLY, r] * diag[1, r]
-        iterate(pg.at[0], pu.at[0], pn.at[0])
-        traded.extend(send_g(pn.at[0], 2))
+            pg[0, 0, r] = ext[EARLY, r] * diag[1, r]
+        part_step(0, 0)
 
     def field_part(i):
         arrive(shared[i])
@@ -371,35 +382,45 @@
                 v = u[i, r]
             else:
                 v = uh[i, r if r < HALO else r - ROWS]
-            pg[1 + i, r] = ext[CAP, r] * diag[1, r] * v
-        iterate(pg.at[1 + i], pu.at[1 + i], pn.at[1 + i])
-        traded.extend(send_g(pn.at[1 + i], 3 + i))
+            pg[0, 1 + i, r] = ext[CAP, r] * diag[1, r] * v
+        part_step(0, 1 + i)
 
     source_part()
     field_part(0)
     arrive(moving)
     iterate(g.at[2], u.at[2], z1)
+    shared.append(send_u(2))
     add_products(parts, 2, g.at[2], u.at[2], z1)
     a0[core] = moment_row(parts).reshape(1, 1, 128)
     for c in loads[8:10]:
         c.wait()
     pl.semaphore_wait(reach.at[1], 2)
-    row = all_sum(
-        (a0, a1, a2), 0,
-        (lambda: shared.append(send_u(2)), lambda: field_part(1), lambda: field_part(2)),
-    )
+
+    def beside_plane():
+        field_part(1)
+        field_part(2)
+
+    def beside_z():
+        for n in (0, 1, 2, 3):
+            part_step(1, n)
+
+    row = all_sum((a0, a1, a2), 0, (None, beside_plane, beside_z))
     c1 = coefficients(row.reshape(1, 128))
-    arrive(traded)
+
+    def added(ref, r):
+        return ref[0, r] + c1[0] * ref[1, r] + c1[1] * ref[2, r] + c1[2] * ref[3, r]
+
+    for n in range(4):
+        arrive(traded[1, n])
+    for r in range(SPAN):
+        g[5, r] = added(pg.at[2], r)
+    iterate(g.at[5], u.at[5], z1)
     held = jnp.zeros((LAYERS, COLS), jnp.float32)
-    for r in range(SPAN):
-        g[3, r] = pn[0, r] + c1[0] * pn[1, r] + c1[1] * pn[2, r] + c1[2] * pn[3, r]
-        if r in own_rows:
-            g[5, r] = pg[0, r] + c1[0] * pg[1, r] + c1[1] * pg[2, r] + c1[2] * pg[3, r]
-            u[5, r] = pu[0, r] + c1[0] * pu[1, r] + c1[1] * pu[2, r] + c1[2] * pu[3, r]
-    parts = [None] * 6
-    iterate(g.at[3], u.at[3], g.at[4])
-    moving = send_g(g.at[4], 6)
     for r in own_rows:
+        g[3, r] = added(pg.at[0], r)
+        g[4, r] = added(pg.at[1], r)
+        u[3, r] = added(pu.at[0], r)
+        u[4, r] = added(pu.at[1], r)
         v = c1[0] * u[0, r] + c1[1] * u[1, r] + c1[2] * u[2, r]
         out_late[:, r - HALO, :] = v[:, :COLS]
         held = held + v[:, :COLS] * rate_late[:, r - HALO, :]
@@ -411,16 +432,15 @@
     ]
     stores[0].start()
 
-    add_products(parts, 0, g.at[5], u.at[5], g.at[3])
-    add_products(parts, 1, g.at[3], u.at[3], g.at[4])
+    parts = [None] * 6
+    add_products(parts, 0, g.at[3], u.at[3], g.at[4])
+    add_products(parts, 1, g.at[4], u.at[4], g.at[5])
+    add_products(parts, 2, g.at[5], u.at[5], z1)
     for c in loads[10:]:
         c.wait()
-    arrive(moving)
-    iterate(g.at[4], u.at[4], z1)
-    add_products(parts, 2, g.at[4], u.at[4], z1)
     moments = moment_row(parts)
     terms = [held]
-    for i in (5, 3, 4):
+    for i in (3, 4, 5):
         t = None
         for r in own_rows:
             w = u[i, r][:, :COLS] * rate_early[:, r - HALO, :]
@@ -444,23 +464,35 @@
     sums = lax.dot_general(
         tiles, chosen, (((1,), (1,)), ((), ())), precision=hi, preferred_element_type=f32
     )
+    b0[core, 0] = moments
     for i in range(4):
         s = jnp.sum(sums[i * LAYERS : (i + 1) * LAYERS], axis=0, keepdims=True)
-        b0[core, 2 * i] = s[:, :128]
-        b0[core, 2 * i + 1] = s[:, 128:]
-    b0[core, 8] = moments
-
-    total = all_sum((b0, b1, b2), 3)
-    c2 = coefficients(total[8])
+        b0[core, 1 + 2 * i] = s[:, :128]
+        b0[core, 2 + 2 * i] = s[:, 128:]
+
+    both = group_sum(b0, core, core_peer, 2, sum_send.at[3], sum_recv.at[3])
+    xy = y * 4 + x
+    b1[xy, 0] = both[0]
+    for i in range(4):
+        b1[xy, 1 + i] = jnp.where(core == 0, both[1 + i], both[5 + i])
+    b2[z] = group_sum(b1, xy, plane_peers, 16, sum_send.at[4], sum_recv.at[4])
+    total = group_sum(b2, z, z_peers, 16, sum_send.at[5], sum_recv.at[5])
+    c2 = coefficients(total[0])
     for h in range(2):
-        out_bank[:, h * 128 : (h + 1) * 128] = (
-            total[h] + c2[0] * total[2 + h] + c2[1] * total[4 + h] + c2[2] * total[6 + h]
-        )
-    for r in range(ROWS):
-        e = HALO + r
-        v = c2[0] * u[5, e] + c2[1] * u[3, e] + c2[2] * u[4, e]
-        out_early[:, r, :] = v[:, :COLS]
-    stores[1].start()
+        first_half = total[1 + h] + c2[0] * total[3 + h]
+        second_half = c2[1] * total[1 + h] + c2[2] * total[3 + h]
+        b3[core, h] = jnp.where(core == 0, first_half, second_half)
+
+    def write_early():
+        for r in range(ROWS):
+            e = HALO + r
+            v = c2[0] * u[3, e] + c2[1] * u[4, e] + c2[2] * u[5, e]
+            out_early[:, r, :] = v[:, :COLS]
+        stores[1].start()
+
+    bank_rows = group_sum(b3, core, core_peer, 2, sum_send.at[6], sum_recv.at[6], write_early)
+    out_bank[:, :128] = bank_rows[0]
+    out_bank[:, 128:] = bank_rows[1]
     stores[2].start()
     for c in halo:
         c.wait_send()
@@ -526,27 +558,27 @@
             pltpu.VMEM((6,) + wide, f32),
             pltpu.VMEM((6,) + wide, f32),
             pltpu.VMEM((3, 2 * HALO, LAYERS, WIDE), f32),
-            pltpu.VMEM((4,) + wide, f32),
-            pltpu.VMEM((4,) + wide, f32),
-            pltpu.VMEM((4,) + wide, f32),
+            pltpu.VMEM((3, 4) + wide, f32),
+            pltpu.VMEM((2, 4) + wide, f32),
             pltpu.VMEM(wide, f32),
             pltpu.VMEM(wide, f32),
             pltpu.VMEM((2, 1, 1, 128), f32),
             pltpu.VMEM((16, 1, 1, 128), f32),
             pltpu.VMEM((16, 1, 1, 128), f32),
             pltpu.VMEM((2, 9, 1, 128), f32),
-            pltpu.VMEM((16, 9, 1, 128), f32),
-            pltpu.VMEM((16, 9, 1, 128), f32),
+            pltpu.VMEM((16, 5, 1, 128), f32),
+            pltpu.VMEM((16, 5, 1, 128), f32),
+            pltpu.VMEM((2, 2, 1, 128), f32),
             dma((11,)),
             dma((3,)),
             dma((19,)),
             dma((19,)),
-            dma((7, 2)),
-            dma((7, 2)),
+            dma((10, 2)),
+            dma((10, 2)),
             dma((3, 2)),
             dma((3, 2)),
-            dma((6,)),
-            dma((6,)),
+            dma((7,)),
+            dma((7,)),
             pltpu.SemaphoreType.REGULAR((2,)),
         ],
         compiler_params=pltpu.CompilerParams(

time: 66.7 us -> 67.9 us (1.018)
  Pallas kernels: 65.6 us -> 67 us
    pallas_call x1, Pallas kernels: 64.2 us -> 65.6 us  [on_device(): pl.pallas_call(kernel, out_shape=shapes, in_specs=[hbm] * 11, out_specs=(...]
where the time goes in v5:
time: 67.9 us; the launch traced here: 67.6 us
  Pallas kernels  67 us (99%)
    pallas_call x1, Pallas kernels, on_device(): pl.pallas_call(kernel, out_shape=shapes, in_specs=[hbm] * 11, out_specs=(...  65.6 us
    pallas_call x1, Pallas kernels, on_device(): pl.pallas_call(finish, out_shape=shapes, in_specs=[hbm] * 3, out_specs=(h...  1.44 us

profile of v5, /device:TPU:1, one launch (start us, length us, event | category | flops | bytes accessed | tf_op | source)
XLA Modules:
  0.0 67.6 jit_solution(16363634952626841383)
XLA Ops:
  0.6 65.6 %adjoint_steps.1 = (f32[8,4,256]{2,1,0:T(4,128)}, f32[8,4,256]{2,1,0:T(4,128)}, f32[1,256]{1,0:T(1,128)}) custom-call(f32[8,4,256]{2,1,0:T(4,128)} %cond_x_in.1, f32[8,4,256]{2,1,0:T(4,128)} %cond_y_in.1, f32[8,4,256]{2,1,0:T(4,128)} %via_in.1, f32[8,4,256]{2,1,0:T(4,128)} %cap_in.1, s32[4,256]{1,0:T(4,128)} %cls_in.1, s32[8,8]{1,0:T(8,128)} %mask_in.1, ...), custom_call_target="tpu_custom_call" | custom-call | tf_op jit(solution)/shard_map/adjoint_steps/pallas_call | solution.py:534
  66.2 1.4 %write_results.1 = (f32[8,4,256]{2,1,0:T(4,128)}, f32[8,4,256]{2,1,0:T(4,128)}, f32[1,256]{1,0:T(1,128)}) custom-call(f32[8,4,256]{2,1,0:T(4,128)} %get-tuple-element.9.late, f32[8,4,256]{2,1,0:T(4,128)} %get-tuple-element.10.early, f32[1,256]{1,0:T(1,128)} %get-tuple-element.11.bank), custom_call_target="tpu_custom_call" | custom-call | tf_op jit(solution)/shard_map/write_results/pallas_call | solution.py:592

commit v6 on v5

--- a/solution.py
+++ b/solution.py
@@ -100,7 +100,7 @@
     late_out, early_out, bank_out,
     out_late, out_early, out_bank, cond_x, cond_y, via, cap, cls, mask, bank, late, early, rate_late, rate_early,
     ext, pack_r, pack_l, col_r, col_l, early_r, early_l, sx, sx_r, sx_l, coef, diag, g, u, uh, pg, pu, z1, z2,
-    a0, a1, a2, b0, b1, b2, b3,
+    a0, a1, a2, b0, b1, b2,
     load_sem, store_sem, halo_send, halo_recv, mid_send, mid_recv, ush_send, ush_recv, sum_send, sum_recv, reach,
 ):
     loads = [
@@ -464,35 +464,23 @@
     sums = lax.dot_general(
         tiles, chosen, (((1,), (1,)), ((), ())), precision=hi, preferred_element_type=f32
     )
-    b0[core, 0] = moments
     for i in range(4):
         s = jnp.sum(sums[i * LAYERS : (i + 1) * LAYERS], axis=0, keepdims=True)
-        b0[core, 1 + 2 * i] = s[:, :128]
-        b0[core, 2 + 2 * i] = s[:, 128:]
-
-    both = group_sum(b0, core, core_peer, 2, sum_send.at[3], sum_recv.at[3])
-    xy = y * 4 + x
-    b1[xy, 0] = both[0]
-    for i in range(4):
-        b1[xy, 1 + i] = jnp.where(core == 0, both[1 + i], both[5 + i])
-    b2[z] = group_sum(b1, xy, plane_peers, 16, sum_send.at[4], sum_recv.at[4])
-    total = group_sum(b2, z, z_peers, 16, sum_send.at[5], sum_recv.at[5])
-    c2 = coefficients(total[0])
+        b0[core, 2 * i] = s[:, :128]
+        b0[core, 2 * i + 1] = s[:, 128:]
+    b0[core, 8] = moments
+
+    total = all_sum((b0, b1, b2), 3)
+    c2 = coefficients(total[8])
     for h in range(2):
-        first_half = total[1 + h] + c2[0] * total[3 + h]
-        second_half = c2[1] * total[1 + h] + c2[2] * total[3 + h]
-        b3[core, h] = jnp.where(core == 0, first_half, second_half)
-
-    def write_early():
-        for r in range(ROWS):
-            e = HALO + r
-            v = c2[0] * u[3, e] + c2[1] * u[4, e] + c2[2] * u[5, e]
-            out_early[:, r, :] = v[:, :COLS]
-        stores[1].start()
-
-    bank_rows = group_sum(b3, core, core_peer, 2, sum_send.at[6], sum_recv.at[6], write_early)
-    out_bank[:, :128] = bank_rows[0]
-    out_bank[:, 128:] = bank_rows[1]
+        out_bank[:, h * 128 : (h + 1) * 128] = (
+            total[h] + c2[0] * total[2 + h] + c2[1] * total[4 + h] + c2[2] * total[6 + h]
+        )
+    for r in range(ROWS):
+        e = HALO + r
+        v = c2[0] * u[3, e] + c2[1] * u[4, e] + c2[2] * u[5, e]
+        out_early[:, r, :] = v[:, :COLS]
+    stores[1].start()
     stores[2].start()
     for c in halo:
         c.wait_send()
@@ -566,9 +554,8 @@
             pltpu.VMEM((16, 1, 1, 128), f32),
             pltpu.VMEM((16, 1, 1, 128), f32),
             pltpu.VMEM((2, 9, 1, 128), f32),
-            pltpu.VMEM((16, 5, 1, 128), f32),
-            pltpu.VMEM((16, 5, 1, 128), f32),
-            pltpu.VMEM((2, 2, 1, 128), f32),
+            pltpu.VMEM((16, 9, 1, 128), f32),
+            pltpu.VMEM((16, 9, 1, 128), f32),
             dma((11,)),
             dma((3,)),
             dma((19,)),

time: 67.9 us -> 66.3 us (0.976)
  Pallas kernels: 67 us -> 65.4 us
    pallas_call x1, Pallas kernels: 65.6 us -> 63.9 us  [on_device(): pl.pallas_call(kernel, out_shape=shapes, in_specs=[hbm] * 11, out_specs=(...]
where the time goes in v6:
time: 66.3 us; the launch traced here: 66 us
  Pallas kernels  65.4 us (99%)
    pallas_call x1, Pallas kernels, on_device(): pl.pallas_call(kernel, out_shape=shapes, in_specs=[hbm] * 11, out_specs=(...  63.9 us
    pallas_call x1, Pallas kernels, on_device(): pl.pallas_call(finish, out_shape=shapes, in_specs=[hbm] * 3, out_specs=(h...  1.44 us

profile of v6, /device:TPU:1, one launch (start us, length us, event | category | flops | bytes accessed | tf_op | source)
XLA Modules:
  0.0 66.0 jit_solution(6477615227824419101)
XLA Ops:
  0.6 63.9 %adjoint_steps.1 = (f32[8,4,256]{2,1,0:T(4,128)}, f32[8,4,256]{2,1,0:T(4,128)}, f32[1,256]{1,0:T(1,128)}) custom-call(f32[8,4,256]{2,1,0:T(4,128)} %cond_x_in.1, f32[8,4,256]{2,1,0:T(4,128)} %cond_y_in.1, f32[8,4,256]{2,1,0:T(4,128)} %via_in.1, f32[8,4,256]{2,1,0:T(4,128)} %cap_in.1, s32[4,256]{1,0:T(4,128)} %cls_in.1, s32[8,8]{1,0:T(8,128)} %mask_in.1, ...), custom_call_target="tpu_custom_call" | custom-call | tf_op jit(solution)/shard_map/adjoint_steps/pallas_call | solution.py:522
  64.6 1.4 %write_results.1 = (f32[8,4,256]{2,1,0:T(4,128)}, f32[8,4,256]{2,1,0:T(4,128)}, f32[1,256]{1,0:T(1,128)}) custom-call(f32[8,4,256]{2,1,0:T(4,128)} %get-tuple-element.9.late, f32[8,4,256]{2,1,0:T(4,128)} %get-tuple-element.10.early, f32[1,256]{1,0:T(1,128)} %get-tuple-element.11.bank), custom_call_target="tpu_custom_call" | custom-call | tf_op jit(solution)/shard_map/write_results/pallas_call | solution.py:579

commit v7 on v6

--- a/solution.py
+++ b/solution.py
@@ -111,9 +111,6 @@
             (rate_late_in, rate_late), (rate_early_in, rate_early),
         ))
     ]
-    for c in loads:
-        c.start()
-
     lay = lax.axis_index("layer")
     til = lax.axis_index("tile")
     lays = lax.axis_size("layer")
@@ -140,10 +137,18 @@
     ]
 
     barrier = pltpu.get_barrier_semaphore()
-    greet = [at(dl, dt) for dt in (-2, -1, 0, 1, 2) for dl in (-1, 0, 1) if (dl, dt) != (0, 0)]
-    greet += plane_peers + [at(0, 4 * dz) for dz in (-2, 2, -1, 1)]
-    for d in greet:
-        pl.semaphore_signal(barrier, inc=1, device_id=d, device_id_type=MESH)
+    near_peers = [at(dl, dt) for dt in (1, -1, 0, 2, -2) for dl in (0, 1, -1) if (dl, dt) != (0, 0)]
+    near_peers += [at(0, 4 * dz) for dz in (-2, 2, -1, 1)]
+    greet = near_peers + plane_peers
+
+    def hello(peers):
+        for d in peers:
+            pl.semaphore_signal(barrier, inc=1, device_id=d, device_id_type=MESH)
+
+    hello(near_peers)
+    for c in loads:
+        c.start()
+    hello(plane_peers)
 
     lane = lax.broadcasted_iota(jnp.int32, (LAYERS, COLS), 1)
     layer = lax.broadcasted_iota(jnp.int32, (LAYERS, COLS), 0)
@@ -470,7 +475,12 @@
         b0[core, 2 * i + 1] = s[:, 128:]
     b0[core, 8] = moments
 
-    total = all_sum((b0, b1, b2), 3)
+    def settle():
+        for c in halo + pending:
+            c.wait_send()
+        pending.clear()
+
+    total = all_sum((b0, b1, b2), 3, (None, None, settle))
     c2 = coefficients(total[8])
     for h in range(2):
         out_bank[:, h * 128 : (h + 1) * 128] = (
@@ -482,8 +492,6 @@
         out_early[:, r, :] = v[:, :COLS]
     stores[1].start()
     stores[2].start()
-    for c in halo:
-        c.wait_send()
     for c in pending:
         c.wait_send()
     for c in stores:

time: 66.3 us -> 66.4 us (level)
  no operation moved by 1% of the time
where the time goes in v7:
time: 66.4 us; the launch traced here: 66.1 us
  Pallas kernels  65.5 us (99%)
    pallas_call x1, Pallas kernels, on_device(): pl.pallas_call(kernel, out_shape=shapes, in_specs=[hbm] * 11, out_specs=(...  64 us
    pallas_call x1, Pallas kernels, on_device(): pl.pallas_call(finish, out_shape=shapes, in_specs=[hbm] * 3, out_specs=(h...  1.44 us

profile of v7, /device:TPU:1, one launch (start us, length us, event | category | flops | bytes accessed | tf_op | source)
XLA Modules:
  0.0 66.1 jit_solution(7176178914302372216)
XLA Ops:
  0.6 64.0 %adjoint_steps.1 = (f32[8,4,256]{2,1,0:T(4,128)}, f32[8,4,256]{2,1,0:T(4,128)}, f32[1,256]{1,0:T(1,128)}) custom-call(f32[8,4,256]{2,1,0:T(4,128)} %cond_x_in.1, f32[8,4,256]{2,1,0:T(4,128)} %cond_y_in.1, f32[8,4,256]{2,1,0:T(4,128)} %via_in.1, f32[8,4,256]{2,1,0:T(4,128)} %cap_in.1, s32[4,256]{1,0:T(4,128)} %cls_in.1, s32[8,8]{1,0:T(8,128)} %mask_in.1, ...), custom_call_target="tpu_custom_call" | custom-call | tf_op jit(solution)/shard_map/adjoint_steps/pallas_call | solution.py:530
  64.7 1.4 %write_results.1 = (f32[8,4,256]{2,1,0:T(4,128)}, f32[8,4,256]{2,1,0:T(4,128)}, f32[1,256]{1,0:T(1,128)}) custom-call(f32[8,4,256]{2,1,0:T(4,128)} %get-tuple-element.9.late, f32[8,4,256]{2,1,0:T(4,128)} %get-tuple-element.10.early, f32[1,256]{1,0:T(1,128)} %get-tuple-element.11.bank), custom_call_target="tpu_custom_call" | custom-call | tf_op jit(solution)/shard_map/write_results/pallas_call | solution.py:587
